TPU v7x, 32 devices: a whole 2x2x4 slice. The times are simulated.
32 devices in a mesh: groups: 2 (over x), ep: 16 (over z, y, core).
Axes of the slice: x: 2, y: 2, z: 4, core: 2. Of those that a mesh axis runs over, the one named last changes fastest.
Arguments:
- hidden_in: bfloat16 [1024, 2048], P(('groups', 'ep')), parts along dimension 0, may hold values from -6 to 6
- queries: bfloat16 [1024, 2048], P(('groups', 'ep')), parts along dimension 0, may hold values from -400 to 400
- stored_keys: bfloat16 [1024, 64, 256], P(('groups', 'ep')), parts along dimension 0, may hold values from -6 to 6
- stored_values: bfloat16 [1024, 64, 256], P(('groups', 'ep')), parts along dimension 0, may hold values from -6 to 6
- stored_lengths: int32 [1024], P(('groups', 'ep')), parts along dimension 0, may hold values from 2 to 64, as said below
- norm_gain: float32 [2048], replicated, may hold values from 0.25 to 1.75
- expert_ids: int32 [1024, 8], P(('groups', 'ep')), parts along dimension 0, may hold values from 0 to 15, all different within a row; in each aligned block of 16 rows (0 to 15, 16 to 31, ...) at most 12 rows name the same one
- gate_weights: float32 [1024, 8], P(('groups', 'ep')), parts along dimension 0, may hold values from 0.05 to 1
- w_gate: bfloat16 [16, 2048, 768], P('ep'), may hold values from -0.125 to 0.125
- w_up: bfloat16 [16, 2048, 768], P('ep'), may hold values from -0.125 to 0.125
- w_down: bfloat16 [16, 768, 2048], P('ep'), may hold values from -0.21875 to 0.21875
Outputs:
- layer_out: bfloat16 [1024, 2048], P(('groups', 'ep')), parts along dimension 0
There are 2 independent parts, one for each index of `groups`. A program takes and returns all parts, laid end to end along the dimension named above; an argument that names none is the same for every part. Nothing has to cross between parts.
Inputs may be any that keep to these rules, and one draw needn't show every extreme that they name: `expert_ids`: every row names 8 different experts. In each aligned block of 16 rows (one micro-batch of one device, micro-batches in order within a device's rows) no expert is named by more than 12 rows, a bound that some block reaches. `stored_lengths`: the largest value 64 is taken by some request.
All inputs are finite; a program needn't handle non-finite values.
Results may differ from a plain program's by a relative error of at most 0.0059.
Values may be sent and summed in bfloat16 or wider, within the bound.
A program may use at most 64 MiB of HBM per device.

v0:
```python
import math

import jax
import jax.numpy as jnp
from jax import lax
from jax.sharding import PartitionSpec as P

QUERY_HEADS = 16
KEY_VALUE_HEADS = 2
MB = 2
MB_ROWS = 16


def cached_attention(queries, stored_keys, stored_values, stored_lengths, heads, kv_heads):
    row_count = queries.shape[0]
    slots = stored_keys.shape[1]
    head_size = queries.shape[1] // heads
    query_head_rows = queries.reshape(row_count, kv_heads, heads // kv_heads, head_size)
    key_head_rows = stored_keys.reshape(row_count, slots, kv_heads, head_size)
    value_head_rows = stored_values.reshape(row_count, slots, kv_heads, head_size)
    scores = jnp.einsum(
        "nkgd,nckd->nkgc", query_head_rows, key_head_rows, preferred_element_type=jnp.float32
    ) / math.sqrt(head_size)
    visible = jnp.arange(slots, dtype=jnp.int32)[None, :] < stored_lengths[:, None]
    visible = visible[:, None, None, :]
    scores = jnp.where(visible, scores, -1e30)
    top_score = jnp.max(scores, axis=-1, keepdims=True)
    expo = jnp.where(visible, jnp.exp(scores - top_score), 0.0)
    probs = (expo / jnp.sum(expo, axis=-1, keepdims=True)).astype(jnp.bfloat16)
    attention_output = jnp.einsum(
        "nkgc,nckd->nkgd", probs, value_head_rows, preferred_element_type=jnp.float32
    )
    return attention_output.reshape(row_count, heads * head_size)


def expert_work(blocks, w_gate, w_up, w_down):
    gate_part = jnp.einsum("secd,edf->secf", blocks, w_gate, preferred_element_type=jnp.float32)
    up_part = jnp.einsum("secd,edf->secf", blocks, w_up, preferred_element_type=jnp.float32)
    inner = (jax.nn.silu(gate_part) * up_part).astype(jnp.bfloat16)
    return jnp.einsum("secf,efd->secd", inner, w_down, preferred_element_type=jnp.float32).astype(
        jnp.bfloat16
    )


def routed(normed, expert_ids, gate_weights, w_gate, w_up, w_down, capacity):
    devices = lax.axis_size("ep")
    local_count = w_gate.shape[0]
    experts = devices * local_count
    width = normed.shape[1]
    row_count, top_count = expert_ids.shape
    flat_ids = expert_ids.reshape(-1)
    onehot_table = (flat_ids[:, None] == jnp.arange(experts, dtype=jnp.int32)[None, :]).astype(
        jnp.int32
    )
    before = jnp.cumsum(onehot_table, axis=0) - onehot_table
    slot_index = jnp.sum(before * onehot_table, axis=1)
    target = flat_ids * capacity + slot_index
    target_rows = target.reshape(row_count, top_count)
    placing = jnp.sum(
        (
            target_rows[:, :, None]
            == jnp.arange(experts * capacity, dtype=jnp.int32)[None, None, :]
        ).astype(jnp.float32),
        axis=1,
    ).astype(jnp.bfloat16)
    buffer = jnp.einsum("tp,td->pd", placing, normed, preferred_element_type=jnp.float32).astype(
        jnp.bfloat16
    )
    buffer = buffer.reshape(experts, capacity, width)
    arrived = lax.all_to_all(buffer, "ep", split_axis=0, concat_axis=0, tiled=True)
    item_count = arrived.shape[1]
    blocks = arrived.reshape(devices, local_count, item_count, width)
    finished = expert_work(blocks, w_gate, w_up, w_down).reshape(experts, item_count, width)
    results = lax.all_to_all(finished, "ep", split_axis=0, concat_axis=0, tiled=True)
    picked = jnp.take(results.reshape(experts * capacity, width), target, axis=0)
    picked = picked.reshape(row_count, top_count, width).astype(jnp.float32)
    return jnp.sum(picked * gate_weights[:, :, None], axis=1)


def layer_rows(
    hidden_in,
    queries,
    stored_keys,
    stored_values,
    stored_lengths,
    norm_gain,
    expert_ids,
    gate_weights,
    w_gate,
    w_up,
    w_down,
    capacity,
):
    attention_output = cached_attention(
        queries, stored_keys, stored_values, stored_lengths, QUERY_HEADS, KEY_VALUE_HEADS
    )
    resid = hidden_in.astype(jnp.float32) + attention_output
    mean_square = jnp.mean(resid * resid, axis=-1, keepdims=True)
    normed = (resid * lax.rsqrt(mean_square + 1e-06) * norm_gain[None, :]).astype(jnp.bfloat16)
    mixture = routed(normed, expert_ids, gate_weights, w_gate, w_up, w_down, capacity)
    return (resid + mixture).astype(jnp.bfloat16)


def local(
    hidden_in,
    queries,
    stored_keys,
    stored_values,
    stored_lengths,
    norm_gain,
    expert_ids,
    gate_weights,
    w_gate,
    w_up,
    w_down,
):
    experts = lax.axis_size("ep") * w_gate.shape[0]
    top_count = expert_ids.shape[1]
    capacity = max(2, 3 * MB_ROWS * top_count // (2 * experts))
    return layer_rows(
        hidden_in,
        queries,
        stored_keys,
        stored_values,
        stored_lengths,
        norm_gain,
        expert_ids,
        gate_weights,
        w_gate,
        w_up,
        w_down,
        MB * capacity,
    )


def solution(mesh):
    in_specs = (
        P(("groups", "ep"), None),
        P(("groups", "ep"), None),
        P(("groups", "ep"), None, None),
        P(("groups", "ep"), None, None),
        P(("groups", "ep")),
        P(),
        P(("groups", "ep"), None),
        P(("groups", "ep"), None),
        P("ep", None, None),
        P("ep", None, None),
        P("ep", None, None),
    )
    out_specs = P(("groups", "ep"), None)
    return jax.shard_map(local, mesh=mesh, in_specs=in_specs, out_specs=out_specs, check_vma=False)
```

profile of v0, /device:TPU:13, one launch (start us, length us, event | category | flops | bytes accessed | tf_op | source)
XLA Modules:
  0.0 114.2 jit_solution(12084656877042410913)
XLA Ops:
  0.0 0.0 copy-start
  0.0 0.9 copy.26
  0.9 0.1 eq.39
  1.0 0.1 reshape.141
  1.1 0.6 reduce-window.6
  1.7 0.2 slice_reduce_fusion
  1.9 0.1 fusion.43
  2.0 0.1 reduce_sum.51
  2.1 0.6 compare_and_fusion
  2.7 0.8 convert_reduce_fusion
  3.5 0.9 copy.34
  4.4 0.7 iota_compare_fusion.3
  5.2 3.3 %fusion.48 = (f32[32,2,8]{2,1,0:T(2,128)}, f32[32,2,8,64]{3,2,1,0:T(8,128)}) fusion(pred[32,64]{1,0:T(8,128)(4,1)S(1)} %iota_compare_fusion.3, bf16[32,2,8,128]{3,2,1,0:T(8,128)(2,1)S(1)} %bitcast.117, bf16[32,64,256]{2,1,0:T(8,128)(2,1)} %param.13), kind=kOutput, calls=%fused_computation.57 | convolution fusion | flops 8552511 | bytes 1314816 | tf_op jit(solution)/shard_map/sub | solution.py:28
  8.5 1.8 %fusion.29 = f32[32,2,8,128]{3,2,1,0:T(8,128)S(1)} fusion(f32[32,2,8,64]{3,2,1,0:T(8,128)} %get-tuple-element.8, f32[32,2,8]{2,1,0:T(2,128)} %get-tuple-element.7, bf16[32,64,256]{2,1,0:T(8,128)(2,1)} %param.14), kind=kOutput, calls=%fused_computation.21 | convolution fusion | flops 8454144 | bytes 1443840 | tf_op jit(solution)/shard_map/nkgc,nckd->nkgd/dot_general | solution.py:30
  10.3 0.0 copy-done.2
  10.3 0.2 multiply_reduce_fusion.1
  10.5 0.6 convolution_convert_fusion
  11.1 0.0 copy-start.6
  11.1 42.7 %all_to_all.10 = bf16[16,24,2048]{2,1,0:T(8,128)(2,1)S(1)} all-to-all(bf16[16,24,2048]{2,1,0:T(8,128)(2,1)S(1)} %bitcast.112), channel_id=1, replica_groups=mesh['groups'=2,'ep'=16] {'ep'}, dimensions={0} | all-to-all | bytes 3145728 | tf_op jit(solution)/shard_map/all_to_all | solution.py:70
  53.8 1.1 %copy-done.1 = bf16[16,24,2048]{2,1,0:T(8,128)(2,1)} copy-done((bf16[16,24,2048]{2,1,0:T(8,128)(2,1)}, bf16[16,24,2048]{2,1,0:T(8,128)(2,1)S(1)}, u32[]{:S(2)}) %copy-start.1) | copy-done | bytes 1572888
  55.0 2.5 %fusion.10 = f32[16,1,24,768]{3,2,0,1:T(8,128)} fusion(bf16[16,24,2048]{2,1,0:T(8,128)(2,1)S(1)} %all_to_all.10, bf16[1,2048,768]{2,1,0:T(8,128)(2,1)S(1)} %copy-done.6), kind=kOutput, calls=%fused_computation.11 | convolution fusion | flops 1207959552 | bytes 5898240 | tf_op jit(solution)/shard_map/secd,edf->secf/dot_general | solution.py:37
  57.4 6.9 %fusion.7 = bf16[16,24,2048]{2,1,0:T(8,128)(2,1)} fusion(bf16[1,768,2048]{2,1,0:T(8,128)(2,1)S(1)} %copy-done, bf16[16,24,2048]{2,1,0:T(8,128)(2,1)} %copy-done.1, bf16[1,2048,768]{2,1,0:T(8,128)(2,1)} %param.20, f32[16,1,24,768]{3,2,0,1:T(8,128)} %fusion.10), kind=kOutput, calls=%fused_computation.8 | convolution fusion | flops 2418475008 | bytes 10616832 | tf_op jit(solution)/shard_map/secf,efd->secd/dot_general | solution.py:40
  64.4 5.0 %all-to-all-start.1 = ((bf16[16,24,2048]{2,1,0:T(8,128)(2,1)}), bf16[16,24,2048]{2,1,0:T(8,128)(2,1)}, u32[]{:S(2)}, u32[]{:S(2)}) async-start(bf16[16,24,2048]{2,1,0:T(8,128)(2,1)} %fusion.7), calls=%async_computation.1 | async-start | bytes 3145728 | tf_op jit(solution)/shard_map/all_to_all | solution.py:74
  69.4 0.6 broadcast_multiply_fusion
  70.0 1.4 %mul.68 = s32[256,1]{0,1:T(1,128)} reshape(s32[32,8]{1,0:T(8,128)} %broadcast_multiply_fusion) | data formatting | bytes 2048 | tf_op jit(solution)/shard_map/mul | solution.py:57
  71.4 0.8 copy.30
  72.2 0.7 compare_select_fusion.1
  72.8 0.6 pad_clamp_fusion
  73.4 32.3 %all-to-all-done.1 = bf16[16,24,2048]{2,1,0:T(8,128)(2,1)} async-done(((bf16[16,24,2048]{2,1,0:T(8,128)(2,1)}), bf16[16,24,2048]{2,1,0:T(8,128)(2,1)}, u32[]{:S(2)}, u32[]{:S(2)}) %all-to-all-start.1) | async-done | bytes 1572896 | tf_op jit(solution)/shard_map/all_to_all | solution.py:74
  105.7 5.1 %gather_fusion = bf16[256,2048]{1,0:T(8,128)(2,1)} fusion(bf16[384,2048]{1,0:T(8,128)(2,1)} %bitcast.17, s32[1024]{0:T(1024)} %pad_clamp_fusion), kind=kCustom, calls=%fused_computation | custom fusion | bytes 2098176 | tf_op jit(solution)/shard_map/jit(_take)/gather | solution.py:75
  110.8 2.7 %multiply_reduce_fusion = f32[32,2048]{1,0:T(8,128)S(1)} fusion(bf16[256,2048]{1,0:T(8,128)(2,1)} %gather_fusion, f32[32,8]{1,0:T(8,128)S(1)} %copy.30, pred[32,8]{1,0:T(8,128)(4,1)} %get-tuple-element.5), kind=kLoop, calls=%fused_computation.10 | loop fusion | flops 2031616 | bytes 1312000 | tf_op jit(solution)/shard_map/reduce_sum | solution.py:77
  113.5 0.8 add_convert_fusion
  (14 shorter events, 0.1 us)
Async XLA Ops:
  0.0 57.4 %copy-start = (bf16[1,768,2048]{2,1,0:T(8,128)(2,1)S(1)}, bf16[1,768,2048]{2,1,0:T(8,128)(2,1)}, u32[]{:S(2)}) copy-start(bf16[1,768,2048]{2,1,0:T(8,128)(2,1)} %param.21) | copy-start | bytes 9437188
  2.0 1.5 %copy-start.4 = (s32[256]{0:T(256)}, s32[256]{0:T(256)S(1)}, u32[]{:S(2)}) copy-start(s32[256]{0:T(256)S(1)} %fusion.43) | copy-start | bytes 3076
  8.5 1.8 %copy-start.2 = (bf16[32,2048]{1,0:T(8,128)(2,1)S(1)}, bf16[32,2048]{1,0:T(8,128)(2,1)}, u32[]{:S(2)}) copy-start(bf16[32,2048]{1,0:T(8,128)(2,1)} %param.11) | copy-start | bytes 393220
  8.5 2.0 %copy-start.3 = (bf16[32,384]{1,0:T(8,128)(2,1)S(1)}, bf16[32,384]{1,0:T(8,128)(2,1)}, u32[]{:S(2)}) copy-start(bf16[32,384]{1,0:T(8,128)(2,1)} %convert_reduce_fusion) | copy-start | bytes 73732
  8.5 2.0 %copy-start.5 = (f32[2048]{0:T(1024)S(1)}, f32[2048]{0:T(1024)}, u32[]{:S(2)}) copy-start(f32[2048]{0:T(1024)} %param.16) | copy-start | bytes 24580
  11.1 43.8 %copy-start.6 = (bf16[1,2048,768]{2,1,0:T(8,128)(2,1)S(1)}, bf16[1,2048,768]{2,1,0:T(8,128)(2,1)}, u32[]{:S(2)}) copy-start(bf16[1,2048,768]{2,1,0:T(8,128)(2,1)} %param.19) | copy-start | bytes 9437188
  53.8 1.1 %copy-start.1 = (bf16[16,24,2048]{2,1,0:T(8,128)(2,1)}, bf16[16,24,2048]{2,1,0:T(8,128)(2,1)S(1)}, u32[]{:S(2)}) copy-start(bf16[16,24,2048]{2,1,0:T(8,128)(2,1)S(1)} %all_to_all.10) | copy-start | bytes 4718596
  64.4 41.3 %all-to-all-start.1 = ((bf16[16,24,2048]{2,1,0:T(8,128)(2,1)}), bf16[16,24,2048]{2,1,0:T(8,128)(2,1)}, u32[]{:S(2)}, u32[]{:S(2)}) async-start(bf16[16,24,2048]{2,1,0:T(8,128)(2,1)} %fusion.7), calls=%async_computation.1 | async-start | bytes 3145728 | tf_op jit(solution)/shard_map/all_to_all | solution.py:74
where the time goes:
time: 115 us; the launch traced here: 114 us
  blocking collectives  42.7 us (37%)
  waiting for transfers between devices  32.3 us (28%)
  matrix products  15.1 us (13%)
  local copies, waits for them, and re-layouts  10.7 us (9%)
  other arithmetic  8.38 us (7%)
  starting transfers between devices  5.05 us (4%)
    all_to_all x1, blocking collectives, routed(): lax.all_to_all(buffer, 'ep', split_axis=0, concat_axis=0, tiled=True)  42.7 us
    all_to_all x1, waiting for transfers between devices, routed(): lax.all_to_all(finished, 'ep', split_axis=0, concat_axis=0, tiled=True)  32.3 us
    dot_general x1, matrix products, expert_work(): jnp.einsum('secf,efd->secd', inner, w_down, preferred_element_type=jnp.fl...  6.91 us
    gather x1, local copies, waits for them, and re-layouts, routed(): jnp.take(results.reshape(experts * capacity, width), target, axis=0)  5.1 us
    all_to_all x1, starting transfers between devices, routed(): lax.all_to_all(finished, 'ep', split_axis=0, concat_axis=0, tiled=True)  5.05 us
    unnamed x17, local copies, waits for them, and re-layouts  3.77 us
    sub x1, matrix products, cached_attention(): expo = jnp.where(visible, jnp.exp(scores - top_score), 0.0)  3.29 us
    reduce_sum x1, other arithmetic, routed(): return jnp.sum(picked * gate_weights[:, :, None], axis=1)  2.66 us
  transfers between devices with their start and end apart: 1, of which 1 were waited for; matrix products, arithmetic and copies ran while one was open for 4% of the time, Pallas kernels for 0%

commit v1 on v0

--- a/solution.py
+++ b/solution.py
@@ -1,8 +1,11 @@
+import functools
 import math
 
 import jax
 import jax.numpy as jnp
 from jax import lax
+from jax.experimental import pallas as pl
+from jax.experimental.pallas import tpu as pltpu
 from jax.sharding import PartitionSpec as P
 
 QUERY_HEADS = 16
@@ -101,6 +104,402 @@
     return (resid + mixture).astype(jnp.bfloat16)
 
 
+LANES = 128
+GROUP = 8
+
+
+def chip_at(position, chips):
+    half = chips // 2
+    return jnp.where(position < half, 2 * position, 2 * (chips - 1 - position) + 1)
+
+
+def position_of(chip, chips):
+    return jnp.where(lax.rem(chip, 2) == 0, chip // 2, chips - 1 - chip // 2)
+
+
+def tile_of(extent, most):
+    return max(t for t in range(LANES, most + 1, LANES) if extent % t == 0)
+
+
+def layer_kernel(
+    devices,
+    heads,
+    kv_heads,
+    hidden_ref,
+    queries_ref,
+    lengths_ref,
+    gain_ref,
+    ids_ref,
+    weights_ref,
+    keys_hbm,
+    values_hbm,
+    gate_hbm,
+    up_hbm,
+    down_hbm,
+    out_ref,
+    keys_ref,
+    values_ref,
+    gate_ref,
+    up_ref,
+    down_ref,
+    resid_ref,
+    rows_ref,
+    inner_ref,
+    own_ref,
+    sibling_ref,
+    outgoing_ref,
+    incoming_ref,
+    kv_sem,
+    w_sem,
+    ring_send,
+    ring_recv,
+    pair_send,
+    pair_recv,
+    back_pair_send,
+    back_pair_recv,
+    back_send,
+    back_recv,
+):
+    chips = devices // 2
+    hops = chips // 2
+    count, width = hidden_ref.shape
+    slots = keys_ref.shape[1]
+    head_size = width // heads
+    per_kv = heads // kv_heads
+    half = count // 2
+    top_count = ids_ref.shape[1]
+    hidden_units = gate_ref.shape[1]
+
+    me = lax.axis_index("ep")
+    core = lax.rem(me, 2)
+    position = position_of(me // 2, chips)
+    right = chip_at(lax.rem(position + 1, chips), chips) * 2 + core
+    left = chip_at(lax.rem(position + chips - 1, chips), chips) * 2 + core
+    sibling = me + 1 - 2 * core
+    onward = (right, left)
+
+    groups = count // GROUP
+    kv_copies = []
+    for i in range(groups):
+        part = pl.ds(i * GROUP, GROUP)
+        for j, (src, dst) in enumerate(((keys_hbm, keys_ref), (values_hbm, values_ref))):
+            copy = pltpu.make_async_copy(src.at[part], dst.at[part], kv_sem.at[i, j])
+            copy.start()
+            kv_copies.append(copy)
+    w_copies = []
+    for j, (src, dst) in enumerate(((gate_hbm, gate_ref), (up_hbm, up_ref), (down_hbm, down_ref))):
+        copy = pltpu.make_async_copy(src.at[0], dst, w_sem.at[j])
+        copy.start()
+        w_copies.append(copy)
+
+    barrier = pltpu.get_barrier_semaphore()
+    for other in (left, right, sibling):
+        pl.semaphore_signal(
+            barrier, inc=1, device_id={"ep": other}, device_id_type=pl.DeviceIdType.MESH
+        )
+
+    scale = 1.0 / math.sqrt(head_size)
+    square_rows = per_kv * GROUP
+    row_id = lax.broadcasted_iota(jnp.int32, (square_rows, GROUP * slots), 0)
+    col_id = lax.broadcasted_iota(jnp.int32, (square_rows, GROUP * slots), 1)
+    same_request = (row_id % GROUP) == (col_id // slots)
+    slot_id = col_id % slots
+    for i in range(groups):
+        kv_copies[2 * i].wait()
+        kv_copies[2 * i + 1].wait()
+        part = pl.ds(i * GROUP, GROUP)
+        lengths = jnp.concatenate([lengths_ref[part, :]] * per_kv, axis=0)
+        visible = same_request & (slot_id < lengths)
+        group_queries = queries_ref[part, :].astype(jnp.float32)
+        hidden = hidden_ref[part, :].astype(jnp.float32)
+        for g in range(kv_heads):
+            lanes = slice(g * head_size, (g + 1) * head_size)
+            first = g * per_kv
+            q = jnp.concatenate(
+                [
+                    group_queries[:, (first + h) * head_size : (first + h + 1) * head_size]
+                    for h in range(per_kv)
+                ],
+                axis=0,
+            ).astype(jnp.bfloat16)
+            k = keys_ref[part, :, lanes].reshape(GROUP * slots, head_size)
+            v = values_ref[part, :, lanes].reshape(GROUP * slots, head_size)
+            scores = (
+                lax.dot_general(q, k, (((1,), (1,)), ((), ())), preferred_element_type=jnp.float32)
+                * scale
+            )
+            scores = jnp.where(visible, scores, -1e30)
+            expo = jnp.where(visible, jnp.exp(scores - jnp.max(scores, axis=-1, keepdims=True)), 0.0)
+            probs = (expo / jnp.sum(expo, axis=-1, keepdims=True)).astype(jnp.bfloat16)
+            attended = jnp.dot(probs, v, preferred_element_type=jnp.float32)
+            for h in range(per_kv):
+                cols = slice((first + h) * head_size, (first + h + 1) * head_size)
+                resid_ref[part, cols] = hidden[:, cols] + attended[h * GROUP : (h + 1) * GROUP, :]
+
+    resid = resid_ref[...]
+    mean_square = jnp.mean(resid * resid, axis=-1, keepdims=True)
+    rows_ref[0:count, 0:width] = (resid * lax.rsqrt(mean_square + 1e-06) * gain_ref[...]).astype(
+        jnp.bfloat16
+    )
+    lane = lax.broadcasted_iota(jnp.int32, (count, LANES), 1)
+    table = jnp.zeros((count, LANES), jnp.float32)
+    for k in range(top_count):
+        chosen = ids_ref[:, k : k + 1]
+        table = table + jnp.where(
+            (lane == chosen) | (lane == chosen + devices), weights_ref[:, k : k + 1], 0.0
+        )
+    coarse = table.astype(jnp.bfloat16)
+    fine = (table - coarse.astype(jnp.float32)).astype(jnp.bfloat16)
+    rows_ref[0:count, width : width + LANES] = jnp.where(
+        lane < devices, coarse.astype(jnp.float32), fine.astype(jnp.float32)
+    ).astype(jnp.bfloat16)
+
+    pl.semaphore_wait(barrier, 3)
+
+    def chunk(s):
+        return 0 if s == 0 else 2 * count + (s - 1) * 4 * count
+
+    def own_rows(s):
+        return 0 if s == 0 else count + (s - 1) * 2 * count
+
+    def half_at(s, direction, h):
+        if s == hops:
+            return chunk(s) + h * half
+        return chunk(s) + direction * count + h * half
+
+    def remote(src, dst, send, recv, other):
+        return pltpu.make_async_remote_copy(
+            src_ref=src,
+            dst_ref=dst,
+            send_sem=send,
+            recv_sem=recv,
+            device_id={"ep": other},
+            device_id_type=pl.DeviceIdType.MESH,
+        )
+
+    def travels(s, direction, h):
+        return s < hops or h == direction
+
+    def ring_copy(s, direction, h):
+        source = h * half if s == 1 else half_at(s - 1, direction, h)
+        return remote(
+            rows_ref.at[pl.ds(source, half)],
+            rows_ref.at[pl.ds(half_at(s, direction, h), half)],
+            ring_send.at[s - 1, direction, h],
+            ring_recv.at[s - 1, direction, h],
+            onward[direction],
+        )
+
+    def pair_copy(s, direction, h):
+        start = half_at(s, direction, h)
+        size = count if s == hops else 2 * count
+        return remote(
+            rows_ref.at[pl.ds(start, half)],
+            rows_ref.at[pl.ds(start + size, half)],
+            pair_send.at[s, direction, h],
+            pair_recv.at[s, direction, h],
+            sibling,
+        )
+
+    parts = [(h, direction) for h in range(2) for direction in range(2)]
+    sent = []
+
+    def go(copy):
+        copy.start()
+        sent.append(copy)
+
+    for h, direction in parts:
+        go(ring_copy(1, direction, h))
+    home = remote(
+        rows_ref.at[pl.ds(0, count)],
+        rows_ref.at[pl.ds(count, count)],
+        pair_send.at[0, 0, 0],
+        pair_recv.at[0, 0, 0],
+        sibling,
+    )
+    go(home)
+
+    f_tile = tile_of(hidden_units, 256)
+    d_tile = tile_of(width, 512)
+
+    def expert(start, size):
+        span = pl.ds(start, size)
+
+        def first(i, carry):
+            cols = pl.ds(pl.multiple_of(i * f_tile, f_tile), f_tile)
+            x = rows_ref[span, 0:width]
+            gate = jnp.dot(x, gate_ref[:, cols], preferred_element_type=jnp.float32)
+            up = jnp.dot(x, up_ref[:, cols], preferred_element_type=jnp.float32)
+            inner_ref[0:size, cols] = (gate / (1.0 + jnp.exp(-gate)) * up).astype(jnp.bfloat16)
+            return carry
+
+        lax.fori_loop(0, hidden_units // f_tile, first, 0)
+        spot = lax.broadcasted_iota(jnp.int32, (size, LANES), 1)
+        both = rows_ref[span, width : width + LANES].astype(jnp.float32)
+        weight = jnp.sum(
+            jnp.where((spot == me) | (spot == me + devices), both, 0.0), axis=-1, keepdims=True
+        )
+
+        def second(i, carry):
+            cols = pl.ds(pl.multiple_of(i * d_tile, d_tile), d_tile)
+            result = jnp.dot(
+                inner_ref[0:size, :], down_ref[:, cols], preferred_element_type=jnp.float32
+            )
+            own_ref[span, cols] = (result * weight).astype(jnp.bfloat16)
+            return carry
+
+        lax.fori_loop(0, width // d_tile, second, 0)
+
+    def back_pair(s):
+        size = count if s in (0, hops) else 2 * count
+        return remote(
+            own_ref.at[pl.ds(chunk(s) + size, size)],
+            sibling_ref.at[pl.ds(own_rows(s), size)],
+            back_pair_send.at[s],
+            back_pair_recv.at[s],
+            sibling,
+        )
+
+    for s in range(1, hops + 1):
+        moving = [(h, direction) for h, direction in parts if travels(s, direction, h)]
+        for h, direction in moving:
+            ring_copy(s, direction, h).wait_recv()
+            if s < hops and travels(s + 1, direction, h):
+                go(ring_copy(s + 1, direction, h))
+            go(pair_copy(s, direction, h))
+        if s == 1:
+            home.wait_recv()
+            for copy in w_copies:
+                copy.wait()
+        for h, direction in moving:
+            pair_copy(s, direction, h).wait_recv()
+        if s == 1:
+            expert(0, chunk(2))
+            go(back_pair(0))
+        else:
+            expert(chunk(s), 2 * count if s == hops else 4 * count)
+        go(back_pair(s))
+
+    def back_copy(s, direction, h):
+        return remote(
+            outgoing_ref.at[direction, s - 1, pl.ds(h * half, half)],
+            incoming_ref.at[direction, s - 1, pl.ds(h * half, half)],
+            back_send.at[s - 1, direction, h],
+            back_recv.at[s - 1, direction, h],
+            onward[1 - direction],
+        )
+
+    for s in range(hops, 0, -1):
+        back_pair(s).wait_recv()
+        for h, direction in parts:
+            if not travels(s, direction, h):
+                continue
+            start = half_at(s, direction, h)
+            offset = start - chunk(s) + own_rows(s)
+            total = own_ref[pl.ds(start, half), :].astype(jnp.float32) + sibling_ref[
+                pl.ds(offset, half), :
+            ].astype(jnp.float32)
+            if s < hops and travels(s + 1, direction, h):
+                back_copy(s + 1, direction, h).wait_recv()
+                total = total + incoming_ref[direction, s, pl.ds(h * half, half), :].astype(
+                    jnp.float32
+                )
+            outgoing_ref[direction, s - 1, pl.ds(h * half, half), :] = total.astype(jnp.bfloat16)
+            go(back_copy(s, direction, h))
+
+    back_pair(0).wait_recv()
+    for h in range(2):
+        span = pl.ds(h * half, half)
+        total = own_ref[span, :].astype(jnp.float32) + sibling_ref[span, :].astype(jnp.float32)
+        total = total + resid_ref[span, :]
+        for direction in range(2):
+            back_copy(1, direction, h).wait_recv()
+            total = total + incoming_ref[direction, 0, span, :].astype(jnp.float32)
+        out_ref[span, :] = total.astype(jnp.bfloat16)
+
+    for copy in sent:
+        copy.wait_send()
+
+
+def gathered_layer(
+    hidden_in,
+    queries,
+    stored_keys,
+    stored_values,
+    stored_lengths,
+    norm_gain,
+    expert_ids,
+    gate_weights,
+    w_gate,
+    w_up,
+    w_down,
+):
+    devices = lax.axis_size("ep")
+    count, width = hidden_in.shape
+    hidden_units = w_gate.shape[2]
+    hops = devices // 4
+    vmem = pl.BlockSpec(memory_space=pltpu.VMEM)
+    hbm = pl.BlockSpec(memory_space=pl.ANY)
+    dma = pltpu.SemaphoreType.DMA
+    bf16 = jnp.bfloat16
+    return pl.pallas_call(
+        functools.partial(layer_kernel, devices, QUERY_HEADS, KEY_VALUE_HEADS),
+        out_shape=jax.ShapeDtypeStruct((count, width), bf16),
+        in_specs=[vmem] * 6 + [hbm] * 5,
+        out_specs=vmem,
+        scratch_shapes=[
+            pltpu.VMEM(stored_keys.shape, bf16),
+            pltpu.VMEM(stored_values.shape, bf16),
+            pltpu.VMEM(w_gate.shape[1:], bf16),
+            pltpu.VMEM(w_up.shape[1:], bf16),
+            pltpu.VMEM(w_down.shape[1:], bf16),
+            pltpu.VMEM((count, width), jnp.float32),
+            pltpu.VMEM((devices * count, width + LANES), bf16),
+            pltpu.VMEM((6 * count, hidden_units), bf16),
+            pltpu.VMEM((devices * count, width), bf16),
+            pltpu.VMEM((devices * count // 2, width), bf16),
+            pltpu.VMEM((2, hops, count, width), bf16),
+            pltpu.VMEM((2, hops, count, width), bf16),
+            dma((count // GROUP, 2)),
+            dma((3,)),
+            dma((hops, 2, 2)),
+            dma((hops, 2, 2)),
+            dma((hops + 1, 2, 2)),
+            dma((hops + 1, 2, 2)),
+            dma((hops + 1,)),
+            dma((hops + 1,)),
+            dma((hops, 2, 2)),
+            dma((hops, 2, 2)),
+        ],
+        compiler_params=pltpu.CompilerParams(
+            collective_id=0, has_side_effects=True, vmem_limit_bytes=48 * 1024 * 1024
+        ),
+        name="gathered_layer",
+    )(
+        hidden_in,
+        queries,
+        stored_lengths[:, None],
+        norm_gain[None, :],
+        expert_ids,
+        gate_weights,
+        stored_keys,
+        stored_values,
+        w_gate,
+        w_up,
+        w_down,
+    )
+
+
+def gather_suits(devices, local_experts, count, top_count):
+    return (
+        local_experts == 1
+        and devices % 8 == 0
+        and 2 * devices <= LANES
+        and count % 32 == 0
+        and 2 * top_count >= devices
+    )
+
+
 def local(
     hidden_in,
     queries,
@@ -114,7 +513,22 @@
     w_up,
     w_down,
 ):
-    experts = lax.axis_size("ep") * w_gate.shape[0]
+    devices = lax.axis_size("ep")
+    if gather_suits(devices, w_gate.shape[0], hidden_in.shape[0], expert_ids.shape[1]):
+        return gathered_layer(
+            hidden_in,
+            queries,
+            stored_keys,
+            stored_values,
+            stored_lengths,
+            norm_gain,
+            expert_ids,
+            gate_weights,
+            w_gate,
+            w_up,
+            w_down,
+        )
+    experts = devices * w_gate.shape[0]
     top_count = expert_ids.shape[1]
     capacity = max(2, 3 * MB_ROWS * top_count // (2 * experts))
     return layer_rows(

time: 115 us -> 57.8 us (0.50)
  the two profiles are of different devices: /device:TPU:13 before, /device:TPU:0 now
where the time goes in v1:
time: 57.8 us; the launch traced here: 57.4 us
  Pallas kernels  47.6 us (82%)
  local copies, waits for them, and re-layouts  9.76 us (17%)
    pallas_call x1, Pallas kernels, gathered_layer(): pl.pallas_call(functools.partial(layer_kernel, devices, QUERY_HEADS, KEY_...  47.6 us
    unnamed x15, local copies, waits for them, and re-layouts  9.02 us

profile of v1, /device:TPU:0, one launch (start us, length us, event | category | flops | bytes accessed | tf_op | source)
XLA Modules:
  0.0 57.4 jit_solution(13000519525722433994)
XLA Ops:
  0.0 0.7 %copy.12.lengths_ref = s32[32,1]{1,0:T(8,128)S(1)} copy(s32[32,1]{0,1:T(1,128)} %bitcast.3) | data formatting | bytes 256 | tf_op jit(solution)/shard_map/broadcast_in_dim | solution.py:481
  0.7 0.8 %copy.13.ids_ref = s32[32,8]{1,0:T(8,128)S(1)} copy(s32[32,8]{0,1:T(8,128)} %param.17) | data formatting | bytes 2048 | tf_op args[6]
  1.5 0.8 %copy.14.weights_ref = f32[32,8]{1,0:T(8,128)S(1)} copy(f32[32,8]{0,1:T(8,128)} %param.18) | data formatting | bytes 2048 | tf_op args[7]
  2.3 0.0 copy-start
  2.3 1.9 %copy-done = bf16[1,2048,768]{2,1,0:T(8,128)(2,1)S(1)} copy-done((bf16[1,2048,768]{2,1,0:T(8,128)(2,1)S(1)}, bf16[1,2048,768]{2,1,0:T(8,128)(2,1)}, u32[]{:S(2)}) %copy-start) | copy-done | bytes 3145752
  4.1 0.0 copy-start.1
  4.2 1.2 %copy-done.1 = bf16[32,64,256]{2,1,0:T(8,128)(2,1)S(1)} copy-done((bf16[32,64,256]{2,1,0:T(8,128)(2,1)S(1)}, bf16[32,64,256]{2,1,0:T(8,128)(2,1)}, u32[]{:S(2)}) %copy-start.1) | copy-done | bytes 1048600
  5.4 0.0 copy-start.2
  5.4 1.2 %copy-done.2 = bf16[32,64,256]{2,1,0:T(8,128)(2,1)S(1)} copy-done((bf16[32,64,256]{2,1,0:T(8,128)(2,1)S(1)}, bf16[32,64,256]{2,1,0:T(8,128)(2,1)}, u32[]{:S(2)}) %copy-start.2) | copy-done | bytes 1048600
  6.6 0.0 copy-start.3
  6.6 0.9 %copy-done.3 = bf16[32,2048]{1,0:T(8,128)(2,1)S(1)} copy-done((bf16[32,2048]{1,0:T(8,128)(2,1)S(1)}, bf16[32,2048]{1,0:T(8,128)(2,1)}, u32[]{:S(2)}) %copy-start.3) | copy-done | bytes 131096
  7.5 0.0 copy-start.4
  7.5 0.9 %copy-done.4 = bf16[32,2048]{1,0:T(8,128)(2,1)S(1)} copy-done((bf16[32,2048]{1,0:T(8,128)(2,1)S(1)}, bf16[32,2048]{1,0:T(8,128)(2,1)}, u32[]{:S(2)}) %copy-start.4) | copy-done | bytes 131096
  8.4 0.0 copy-start.5
  8.4 0.7 %copy-done.5 = f32[2048]{0:T(1024)S(1)} copy-done((f32[2048]{0:T(1024)S(1)}, f32[2048]{0:T(1024)}, u32[]{:S(2)}) %copy-start.5) | copy-done | bytes 8216
  9.1 47.6 %gathered_layer.1 = bf16[32,2048]{1,0:T(8,128)(2,1)S(1)} custom-call(bf16[32,2048]{1,0:T(8,128)(2,1)S(1)} %copy-done.3, bf16[32,2048]{1,0:T(8,128)(2,1)S(1)} %copy-done.4, s32[32,1]{1,0:T(8,128)S(1)} %copy.12.lengths_ref, f32[1,2048]{1,0:T(1,128)S(1)} %bitcast.2, s32[32,8]{1,0:T(8,128)S(1)} %copy.13.ids_ref, f32[32,8]{1,0:T(8,128)S(1)} %copy.14.weights_ref, ...), custom_call_target="tpu_custom_call" | custom-call | tf_op jit(solution)/shard_map/gathered_layer/pallas_call | solution.py:445
  56.7 0.7 %copy.16 = bf16[32,2048]{1,0:T(8,128)(2,1)} copy(bf16[32,2048]{1,0:T(8,128)(2,1)S(1)} %gathered_layer.1) | data formatting | bytes 262144
Async XLA Ops:
  2.3 1.9 %copy-start = (bf16[1,2048,768]{2,1,0:T(8,128)(2,1)S(1)}, bf16[1,2048,768]{2,1,0:T(8,128)(2,1)}, u32[]{:S(2)}) copy-start(bf16[1,2048,768]{2,1,0:T(8,128)(2,1)} %gate_hbm.1) | copy-start | bytes 9437188
  4.1 1.2 %copy-start.1 = (bf16[32,64,256]{2,1,0:T(8,128)(2,1)S(1)}, bf16[32,64,256]{2,1,0:T(8,128)(2,1)}, u32[]{:S(2)}) copy-start(bf16[32,64,256]{2,1,0:T(8,128)(2,1)} %keys_hbm.1) | copy-start | bytes 3145732
  5.4 1.2 %copy-start.2 = (bf16[32,64,256]{2,1,0:T(8,128)(2,1)S(1)}, bf16[32,64,256]{2,1,0:T(8,128)(2,1)}, u32[]{:S(2)}) copy-start(bf16[32,64,256]{2,1,0:T(8,128)(2,1)} %values_hbm.1) | copy-start | bytes 3145732
  6.6 0.9 %copy-start.3 = (bf16[32,2048]{1,0:T(8,128)(2,1)S(1)}, bf16[32,2048]{1,0:T(8,128)(2,1)}, u32[]{:S(2)}) copy-start(bf16[32,2048]{1,0:T(8,128)(2,1)} %hidden_ref.1) | copy-start | bytes 393220
  7.5 0.9 %copy-start.4 = (bf16[32,2048]{1,0:T(8,128)(2,1)S(1)}, bf16[32,2048]{1,0:T(8,128)(2,1)}, u32[]{:S(2)}) copy-start(bf16[32,2048]{1,0:T(8,128)(2,1)} %queries_ref.1) | copy-start | bytes 393220
  8.4 0.7 %copy-start.5 = (f32[2048]{0:T(1024)S(1)}, f32[2048]{0:T(1024)}, u32[]{:S(2)}) copy-start(f32[2048]{0:T(1024)} %param.16) | copy-start | bytes 24580

commit v2 on v1

--- a/solution.py
+++ b/solution.py
@@ -108,13 +108,13 @@
 GROUP = 8
 
 
-def chip_at(position, chips):
-    half = chips // 2
-    return jnp.where(position < half, 2 * position, 2 * (chips - 1 - position) + 1)
-
-
-def position_of(chip, chips):
-    return jnp.where(lax.rem(chip, 2) == 0, chip // 2, chips - 1 - chip // 2)
+def partner(index, bits):
+    place = 1
+    while place <= bits:
+        if bits & place:
+            index = index + (1 - 2 * lax.rem(index // place, 2)) * place
+        place *= 2
+    return index
 
 
 def tile_of(extent, most):
@@ -125,18 +125,23 @@
     devices,
     heads,
     kv_heads,
-    hidden_ref,
-    queries_ref,
+    hidden_hbm,
+    queries_hbm,
     lengths_ref,
-    gain_ref,
-    ids_ref,
-    weights_ref,
+    gain_hbm,
+    ids_hbm,
+    weights_hbm,
     keys_hbm,
     values_hbm,
     gate_hbm,
     up_hbm,
     down_hbm,
     out_ref,
+    hidden_ref,
+    queries_ref,
+    gain_ref,
+    ids_ref,
+    weights_ref,
     keys_ref,
     values_ref,
     gate_ref,
@@ -147,37 +152,53 @@
     inner_ref,
     own_ref,
     sibling_ref,
+    across_ref,
+    across_in_ref,
     outgoing_ref,
     incoming_ref,
+    small_sem,
     kv_sem,
     w_sem,
-    ring_send,
-    ring_recv,
+    line_send,
+    line_recv,
+    cross_send,
+    cross_recv,
     pair_send,
     pair_recv,
     back_pair_send,
     back_pair_recv,
+    back_cross_send,
+    back_cross_recv,
     back_send,
     back_recv,
 ):
-    chips = devices // 2
-    hops = chips // 2
+    line = devices // 4
     count, width = hidden_ref.shape
     slots = keys_ref.shape[1]
     head_size = width // heads
     per_kv = heads // kv_heads
     half = count // 2
-    top_count = ids_ref.shape[1]
+    top_count = ids_ref.shape[0]
     hidden_units = gate_ref.shape[1]
 
     me = lax.axis_index("ep")
-    core = lax.rem(me, 2)
-    position = position_of(me // 2, chips)
-    right = chip_at(lax.rem(position + 1, chips), chips) * 2 + core
-    left = chip_at(lax.rem(position + chips - 1, chips), chips) * 2 + core
-    sibling = me + 1 - 2 * core
-    onward = (right, left)
-
+    sibling = partner(me, 1)
+    opposite = partner(me, 2)
+    along = [None] + [partner(me, 4 * m) for m in range(1, line)]
+
+    small_copies = []
+    for j, (src, dst) in enumerate(
+        (
+            (queries_hbm, queries_ref),
+            (hidden_hbm, hidden_ref),
+            (gain_hbm, gain_ref),
+            (ids_hbm, ids_ref),
+            (weights_hbm, weights_ref),
+        )
+    ):
+        copy = pltpu.make_async_copy(src, dst, small_sem.at[j])
+        copy.start()
+        small_copies.append(copy)
     groups = count // GROUP
     kv_copies = []
     for i in range(groups):
@@ -193,22 +214,28 @@
         w_copies.append(copy)
 
     barrier = pltpu.get_barrier_semaphore()
-    for other in (left, right, sibling):
+    others = [sibling, opposite] + along[1:]
+    for other in others:
         pl.semaphore_signal(
             barrier, inc=1, device_id={"ep": other}, device_id_type=pl.DeviceIdType.MESH
         )
+    for copy in small_copies:
+        copy.wait()
 
     scale = 1.0 / math.sqrt(head_size)
     square_rows = per_kv * GROUP
     row_id = lax.broadcasted_iota(jnp.int32, (square_rows, GROUP * slots), 0)
     col_id = lax.broadcasted_iota(jnp.int32, (square_rows, GROUP * slots), 1)
-    same_request = (row_id % GROUP) == (col_id // slots)
+    column_request = col_id // slots
+    same_request = (row_id % GROUP) == column_request
     slot_id = col_id % slots
     for i in range(groups):
         kv_copies[2 * i].wait()
         kv_copies[2 * i + 1].wait()
         part = pl.ds(i * GROUP, GROUP)
-        lengths = jnp.concatenate([lengths_ref[part, :]] * per_kv, axis=0)
+        lengths = jnp.zeros((square_rows, GROUP * slots), jnp.int32)
+        for r in range(GROUP):
+            lengths = jnp.where(column_request == r, lengths_ref[i * GROUP + r], lengths)
         visible = same_request & (slot_id < lengths)
         group_queries = queries_ref[part, :].astype(jnp.float32)
         hidden = hidden_ref[part, :].astype(jnp.float32)
@@ -241,31 +268,28 @@
     rows_ref[0:count, 0:width] = (resid * lax.rsqrt(mean_square + 1e-06) * gain_ref[...]).astype(
         jnp.bfloat16
     )
+    spare = LANES - count
+    ids = jnp.concatenate([ids_ref[...], jnp.zeros((top_count, spare), jnp.int32)], axis=1)
+    weights = jnp.concatenate([weights_ref[...], jnp.zeros((top_count, spare), jnp.float32)], axis=1)
+    expert_id = lax.broadcasted_iota(jnp.int32, (LANES, LANES), 0)
+    turned = jnp.zeros((LANES, LANES), jnp.float32)
+    for k in range(top_count):
+        chosen = ids[k : k + 1, :]
+        turned = turned + jnp.where(
+            (expert_id == chosen) | (expert_id == chosen + devices), weights[k : k + 1, :], 0.0
+        )
+    table = turned.T[0:count, :]
     lane = lax.broadcasted_iota(jnp.int32, (count, LANES), 1)
-    table = jnp.zeros((count, LANES), jnp.float32)
-    for k in range(top_count):
-        chosen = ids_ref[:, k : k + 1]
-        table = table + jnp.where(
-            (lane == chosen) | (lane == chosen + devices), weights_ref[:, k : k + 1], 0.0
-        )
     coarse = table.astype(jnp.bfloat16)
     fine = (table - coarse.astype(jnp.float32)).astype(jnp.bfloat16)
     rows_ref[0:count, width : width + LANES] = jnp.where(
         lane < devices, coarse.astype(jnp.float32), fine.astype(jnp.float32)
     ).astype(jnp.bfloat16)
 
-    pl.semaphore_wait(barrier, 3)
-
-    def chunk(s):
-        return 0 if s == 0 else 2 * count + (s - 1) * 4 * count
-
-    def own_rows(s):
-        return 0 if s == 0 else count + (s - 1) * 2 * count
-
-    def half_at(s, direction, h):
-        if s == hops:
-            return chunk(s) + h * half
-        return chunk(s) + direction * count + h * half
+    pl.semaphore_wait(barrier, len(others))
+
+    def place(m, j):
+        return (4 * m + j) * count
 
     def remote(src, dst, send, recv, other):
         return pltpu.make_async_remote_copy(
@@ -277,47 +301,41 @@
             device_id_type=pl.DeviceIdType.MESH,
         )
 
-    def travels(s, direction, h):
-        return s < hops or h == direction
-
-    def ring_copy(s, direction, h):
-        source = h * half if s == 1 else half_at(s - 1, direction, h)
+    def rows_copy(source, target, h, sems, other):
         return remote(
-            rows_ref.at[pl.ds(source, half)],
-            rows_ref.at[pl.ds(half_at(s, direction, h), half)],
-            ring_send.at[s - 1, direction, h],
-            ring_recv.at[s - 1, direction, h],
-            onward[direction],
-        )
-
-    def pair_copy(s, direction, h):
-        start = half_at(s, direction, h)
-        size = count if s == hops else 2 * count
-        return remote(
-            rows_ref.at[pl.ds(start, half)],
-            rows_ref.at[pl.ds(start + size, half)],
-            pair_send.at[s, direction, h],
-            pair_recv.at[s, direction, h],
-            sibling,
-        )
-
-    parts = [(h, direction) for h in range(2) for direction in range(2)]
+            rows_ref.at[pl.ds(source + h * half, half)],
+            rows_ref.at[pl.ds(target + h * half, half)],
+            sems[0],
+            sems[1],
+            other,
+        )
+
+    def line_copy(m, h):
+        sems = (line_send.at[m, h], line_recv.at[m, h])
+        return rows_copy(0, place(m, 0), h, sems, along[m])
+
+    def cross_copy(m, h):
+        sems = (cross_send.at[m, h], cross_recv.at[m, h])
+        return rows_copy(place(m, 0), place(m, 1), h, sems, opposite)
+
+    def pair_copy(m, j, h):
+        sems = (pair_send.at[m, j, h], pair_recv.at[m, j, h])
+        return rows_copy(place(m, j), place(m, j + 2), h, sems, sibling)
+
     sent = []
 
     def go(copy):
         copy.start()
         sent.append(copy)
 
-    for h, direction in parts:
-        go(ring_copy(1, direction, h))
-    home = remote(
-        rows_ref.at[pl.ds(0, count)],
-        rows_ref.at[pl.ds(count, count)],
-        pair_send.at[0, 0, 0],
-        pair_recv.at[0, 0, 0],
-        sibling,
-    )
-    go(home)
+    halves = range(2)
+    for m in range(line - 1, 0, -1):
+        for h in halves:
+            go(line_copy(m, h))
+            if m == line - 1:
+                go(cross_copy(0, h))
+    for h in halves:
+        go(pair_copy(0, 0, h))
 
     f_tile = tile_of(hidden_units, 256)
     d_tile = tile_of(width, 512)
@@ -350,71 +368,104 @@
 
         lax.fori_loop(0, width // d_tile, second, 0)
 
-    def back_pair(s):
-        size = count if s in (0, hops) else 2 * count
+    def back_pair(m):
         return remote(
-            own_ref.at[pl.ds(chunk(s) + size, size)],
-            sibling_ref.at[pl.ds(own_rows(s), size)],
-            back_pair_send.at[s],
-            back_pair_recv.at[s],
+            own_ref.at[pl.ds(place(m, 2), 2 * count)],
+            sibling_ref.at[pl.ds(2 * m * count, 2 * count)],
+            back_pair_send.at[m],
+            back_pair_recv.at[m],
             sibling,
         )
 
-    for s in range(1, hops + 1):
-        moving = [(h, direction) for h, direction in parts if travels(s, direction, h)]
-        for h, direction in moving:
-            ring_copy(s, direction, h).wait_recv()
-            if s < hops and travels(s + 1, direction, h):
-                go(ring_copy(s + 1, direction, h))
-            go(pair_copy(s, direction, h))
-        if s == 1:
-            home.wait_recv()
-            for copy in w_copies:
-                copy.wait()
-        for h, direction in moving:
-            pair_copy(s, direction, h).wait_recv()
-        if s == 1:
-            expert(0, chunk(2))
-            go(back_pair(0))
+    def back_cross(m, h):
+        span = pl.ds(m * count + h * half, half)
+        return remote(
+            across_ref.at[span],
+            across_in_ref.at[span],
+            back_cross_send.at[m, h],
+            back_cross_recv.at[m, h],
+            opposite,
+        )
+
+    def back_line(m, h):
+        span = pl.ds(m * count + h * half, half)
+        return remote(
+            outgoing_ref.at[span],
+            incoming_ref.at[span],
+            back_send.at[m, h],
+            back_recv.at[m, h],
+            along[m],
+        )
+
+    def chip_sum(m, j, h):
+        mine = own_ref[pl.ds(place(m, j) + h * half, half), :].astype(jnp.float32)
+        other = sibling_ref[pl.ds((2 * m + j) * count + h * half, half), :].astype(jnp.float32)
+        return mine + other
+
+    def receive_line(m):
+        for h in halves:
+            line_copy(m, h).wait_recv()
+            go(cross_copy(m, h))
+            go(pair_copy(m, 0, h))
+
+    def receive_rest(m):
+        for h in halves:
+            cross_copy(m, h).wait_recv()
+            go(pair_copy(m, 1, h))
+        for j in range(2):
+            for h in halves:
+                pair_copy(m, j, h).wait_recv()
+
+    def work(m):
+        expert(place(m, 0), 4 * count)
+        go(back_pair(m))
+
+    def send_across(m):
+        back_pair(m).wait_recv()
+        for h in halves:
+            across_ref[pl.ds(m * count + h * half, half), :] = chip_sum(m, 1, h).astype(jnp.bfloat16)
+            go(back_cross(m, h))
+
+    def both_sides(m, h):
+        back_cross(m, h).wait_recv()
+        return chip_sum(m, 0, h) + across_in_ref[pl.ds(m * count + h * half, half), :].astype(
+            jnp.float32
+        )
+
+    def send_along(m):
+        for h in halves:
+            outgoing_ref[pl.ds(m * count + h * half, half), :] = both_sides(m, h).astype(
+                jnp.bfloat16
+            )
+            go(back_line(m, h))
+
+    receive_rest(0)
+    for copy in w_copies:
+        copy.wait()
+    work(0)
+    order = list(range(line - 1, 0, -1))
+    for i, m in enumerate(order):
+        if i >= 2:
+            receive_line(m)
+            send_along(order[i - 2])
         else:
-            expert(chunk(s), 2 * count if s == hops else 4 * count)
-        go(back_pair(s))
-
-    def back_copy(s, direction, h):
-        return remote(
-            outgoing_ref.at[direction, s - 1, pl.ds(h * half, half)],
-            incoming_ref.at[direction, s - 1, pl.ds(h * half, half)],
-            back_send.at[s - 1, direction, h],
-            back_recv.at[s - 1, direction, h],
-            onward[1 - direction],
-        )
-
-    for s in range(hops, 0, -1):
-        back_pair(s).wait_recv()
-        for h, direction in parts:
-            if not travels(s, direction, h):
-                continue
-            start = half_at(s, direction, h)
-            offset = start - chunk(s) + own_rows(s)
-            total = own_ref[pl.ds(start, half), :].astype(jnp.float32) + sibling_ref[
-                pl.ds(offset, half), :
-            ].astype(jnp.float32)
-            if s < hops and travels(s + 1, direction, h):
-                back_copy(s + 1, direction, h).wait_recv()
-                total = total + incoming_ref[direction, s, pl.ds(h * half, half), :].astype(
-                    jnp.float32
-                )
-            outgoing_ref[direction, s - 1, pl.ds(h * half, half), :] = total.astype(jnp.bfloat16)
-            go(back_copy(s, direction, h))
-
-    back_pair(0).wait_recv()
-    for h in range(2):
+            receive_line(m)
+        if i >= 1:
+            send_across(order[i - 1])
+        receive_rest(m)
+        work(m)
+    if len(order) >= 2:
+        send_along(order[-2])
+    send_across(order[-1])
+    send_across(0)
+    send_along(order[-1])
+
+    for h in halves:
         span = pl.ds(h * half, half)
-        total = own_ref[span, :].astype(jnp.float32) + sibling_ref[span, :].astype(jnp.float32)
-        total = total + resid_ref[span, :]
-        for direction in range(2):
-            back_copy(1, direction, h).wait_recv()
-            total = total + incoming_ref[direction, 0, span, :].astype(jnp.float32)
+        total = both_sides(0, h) + resid_ref[span, :]
+        for m in order:
+            back_line(m, h).wait_recv()
+            total = total + incoming_ref[pl.ds(m * count + h * half, half), :].astype(jnp.float32)
         out_ref[span, :] = total.astype(jnp.bfloat16)
 
     for copy in sent:
@@ -437,17 +488,24 @@
     devices = lax.axis_size("ep")
     count, width = hidden_in.shape
     hidden_units = w_gate.shape[2]
-    hops = devices // 4
+    line = devices // 4
     vmem = pl.BlockSpec(memory_space=pltpu.VMEM)
-    hbm = pl.BlockSpec(memory_space=pl.ANY)
+    smem = pl.BlockSpec(memory_space=pltpu.SMEM)
+    hbm = pl.BlockSpec(memory_space=pltpu.HBM)
     dma = pltpu.SemaphoreType.DMA
     bf16 = jnp.bfloat16
+    top_count = expert_ids.shape[1]
     return pl.pallas_call(
         functools.partial(layer_kernel, devices, QUERY_HEADS, KEY_VALUE_HEADS),
         out_shape=jax.ShapeDtypeStruct((count, width), bf16),
-        in_specs=[vmem] * 6 + [hbm] * 5,
+        in_specs=[hbm, hbm, smem] + [hbm] * 8,
         out_specs=vmem,
         scratch_shapes=[
+            pltpu.VMEM((count, width), bf16),
+            pltpu.VMEM((count, width), bf16),
+            pltpu.VMEM((1, width), jnp.float32),
+            pltpu.VMEM((top_count, count), jnp.int32),
+            pltpu.VMEM((top_count, count), jnp.float32),
             pltpu.VMEM(stored_keys.shape, bf16),
             pltpu.VMEM(stored_values.shape, bf16),
             pltpu.VMEM(w_gate.shape[1:], bf16),
@@ -455,33 +513,40 @@
             pltpu.VMEM(w_down.shape[1:], bf16),
             pltpu.VMEM((count, width), jnp.float32),
             pltpu.VMEM((devices * count, width + LANES), bf16),
-            pltpu.VMEM((6 * count, hidden_units), bf16),
+            pltpu.VMEM((4 * count, hidden_units), bf16),
             pltpu.VMEM((devices * count, width), bf16),
             pltpu.VMEM((devices * count // 2, width), bf16),
-            pltpu.VMEM((2, hops, count, width), bf16),
-            pltpu.VMEM((2, hops, count, width), bf16),
+            pltpu.VMEM((line * count, width), bf16),
+            pltpu.VMEM((line * count, width), bf16),
+            pltpu.VMEM((line * count, width), bf16),
+            pltpu.VMEM((line * count, width), bf16),
+            dma((5,)),
             dma((count // GROUP, 2)),
             dma((3,)),
-            dma((hops, 2, 2)),
-            dma((hops, 2, 2)),
-            dma((hops + 1, 2, 2)),
-            dma((hops + 1, 2, 2)),
-            dma((hops + 1,)),
-            dma((hops + 1,)),
-            dma((hops, 2, 2)),
-            dma((hops, 2, 2)),
+            dma((line, 2)),
+            dma((line, 2)),
+            dma((line, 2)),
+            dma((line, 2)),
+            dma((line, 2, 2)),
+            dma((line, 2, 2)),
+            dma((line,)),
+            dma((line,)),
+            dma((line, 2)),
+            dma((line, 2)),
+            dma((line, 2)),
+            dma((line, 2)),
         ],
         compiler_params=pltpu.CompilerParams(
-            collective_id=0, has_side_effects=True, vmem_limit_bytes=48 * 1024 * 1024
+            collective_id=0, has_side_effects=True, vmem_limit_bytes=60 * 1024 * 1024
         ),
         name="gathered_layer",
     )(
         hidden_in,
         queries,
-        stored_lengths[:, None],
+        stored_lengths,
         norm_gain[None, :],
-        expert_ids,
-        gate_weights,
+        expert_ids.T,
+        gate_weights.T,
         stored_keys,
         stored_values,
         w_gate,
@@ -493,9 +558,11 @@
 def gather_suits(devices, local_experts, count, top_count):
     return (
         local_experts == 1
-        and devices % 8 == 0
+        and devices >= 8
+        and devices & (devices - 1) == 0
         and 2 * devices <= LANES
         and count % 32 == 0
+        and count <= LANES
         and 2 * top_count >= devices
     )
 

time: 57.8 us -> 59 us (1.021)
  Pallas kernels: 47.6 us -> 57.3 us
  local copies, waits for them, and re-layouts: 9.76 us -> 1.57 us
    pallas_call x1, Pallas kernels: 47.6 us -> 57.3 us  [gathered_layer(): pl.pallas_call(functools.partial(layer_kernel, devices, QUERY_HEADS, KEY_...]
    unnamed x15 -> x1, local copies, waits for them, and re-layouts: 9.02 us -> 1.57 us
    broadcast_in_dim x1 -> x0, local copies, waits for them, and re-layouts: 0.74 us -> none  [gathered_layer(): stored_lengths[:, None]]
where the time goes in v2:
time: 59 us; the launch traced here: 58.9 us
  Pallas kernels  57.3 us (97%)
  local copies, waits for them, and re-layouts  1.57 us (3%)
    pallas_call x1, Pallas kernels, gathered_layer(): pl.pallas_call(functools.partial(layer_kernel, devices, QUERY_HEADS, KEY_...  57.3 us
    unnamed x1, local copies, waits for them, and re-layouts  1.57 us

profile of v2, /device:TPU:0, one launch (start us, length us, event | category | flops | bytes accessed | tf_op | source)
XLA Modules:
  0.0 58.9 jit_solution(7734589342869949919)
XLA Ops:
  0.0 57.3 %gathered_layer.1 = bf16[32,2048]{1,0:T(8,128)(2,1)} custom-call(bf16[32,2048]{1,0:T(8,128)(2,1)} %hidden_hbm.1, bf16[32,2048]{1,0:T(8,128)(2,1)} %queries_hbm.1, s32[32]{0:T(128)} %lengths_ref.1, f32[1,2048]{1,0:T(1,128)} %bitcast.3, s32[8,32]{1,0:T(8,128)} %bitcast.4, f32[8,32]{1,0:T(8,128)} %bitcast.5, bf16[32,64,256]{2,1,0:T(8,128)(2,1)} %keys_hbm.1, ...), custom_call_target="tpu_custom_call" | custom-call | tf_op jit(solution)/shard_map/gathered_layer/pallas_call | solution.py:498
  57.3 1.6 %copy.13 = bf16[32,2048]{1,0:T(8,128)(2,1)} copy(bf16[32,2048]{1,0:T(8,128)(2,1)} %gathered_layer.1) | data formatting | bytes 262144

commit v3 on v1

--- a/solution.py
+++ b/solution.py
@@ -125,18 +125,23 @@
     devices,
     heads,
     kv_heads,
-    hidden_ref,
-    queries_ref,
+    hidden_hbm,
+    queries_hbm,
     lengths_ref,
-    gain_ref,
-    ids_ref,
-    weights_ref,
+    gain_hbm,
+    ids_hbm,
+    weights_hbm,
     keys_hbm,
     values_hbm,
     gate_hbm,
     up_hbm,
     down_hbm,
     out_ref,
+    hidden_ref,
+    queries_ref,
+    gain_ref,
+    ids_ref,
+    weights_ref,
     keys_ref,
     values_ref,
     gate_ref,
@@ -149,6 +154,7 @@
     sibling_ref,
     outgoing_ref,
     incoming_ref,
+    small_sem,
     kv_sem,
     w_sem,
     ring_send,
@@ -167,7 +173,7 @@
     head_size = width // heads
     per_kv = heads // kv_heads
     half = count // 2
-    top_count = ids_ref.shape[1]
+    top_count = ids_ref.shape[0]
     hidden_units = gate_ref.shape[1]
 
     me = lax.axis_index("ep")
@@ -178,6 +184,19 @@
     sibling = me + 1 - 2 * core
     onward = (right, left)
 
+    small_copies = []
+    for j, (src, dst) in enumerate(
+        (
+            (queries_hbm, queries_ref),
+            (hidden_hbm, hidden_ref),
+            (gain_hbm, gain_ref),
+            (ids_hbm, ids_ref),
+            (weights_hbm, weights_ref),
+        )
+    ):
+        copy = pltpu.make_async_copy(src, dst, small_sem.at[j])
+        copy.start()
+        small_copies.append(copy)
     groups = count // GROUP
     kv_copies = []
     for i in range(groups):
@@ -186,29 +205,29 @@
             copy = pltpu.make_async_copy(src.at[part], dst.at[part], kv_sem.at[i, j])
             copy.start()
             kv_copies.append(copy)
-    w_copies = []
-    for j, (src, dst) in enumerate(((gate_hbm, gate_ref), (up_hbm, up_ref), (down_hbm, down_ref))):
-        copy = pltpu.make_async_copy(src.at[0], dst, w_sem.at[j])
-        copy.start()
-        w_copies.append(copy)
-
     barrier = pltpu.get_barrier_semaphore()
-    for other in (left, right, sibling):
+    others = [left, right, sibling]
+    for other in others:
         pl.semaphore_signal(
             barrier, inc=1, device_id={"ep": other}, device_id_type=pl.DeviceIdType.MESH
         )
+    for copy in small_copies:
+        copy.wait()
 
     scale = 1.0 / math.sqrt(head_size)
     square_rows = per_kv * GROUP
     row_id = lax.broadcasted_iota(jnp.int32, (square_rows, GROUP * slots), 0)
     col_id = lax.broadcasted_iota(jnp.int32, (square_rows, GROUP * slots), 1)
-    same_request = (row_id % GROUP) == (col_id // slots)
+    column_request = col_id // slots
+    same_request = (row_id % GROUP) == column_request
     slot_id = col_id % slots
-    for i in range(groups):
+    def attend(i):
         kv_copies[2 * i].wait()
         kv_copies[2 * i + 1].wait()
         part = pl.ds(i * GROUP, GROUP)
-        lengths = jnp.concatenate([lengths_ref[part, :]] * per_kv, axis=0)
+        lengths = jnp.zeros((square_rows, GROUP * slots), jnp.int32)
+        for r in range(GROUP):
+            lengths = jnp.where(column_request == r, lengths_ref[i * GROUP + r], lengths)
         visible = same_request & (slot_id < lengths)
         group_queries = queries_ref[part, :].astype(jnp.float32)
         hidden = hidden_ref[part, :].astype(jnp.float32)
@@ -236,25 +255,31 @@
                 cols = slice((first + h) * head_size, (first + h + 1) * head_size)
                 resid_ref[part, cols] = hidden[:, cols] + attended[h * GROUP : (h + 1) * GROUP, :]
 
-    resid = resid_ref[...]
-    mean_square = jnp.mean(resid * resid, axis=-1, keepdims=True)
-    rows_ref[0:count, 0:width] = (resid * lax.rsqrt(mean_square + 1e-06) * gain_ref[...]).astype(
-        jnp.bfloat16
-    )
+    spare = LANES - count
+    ids = jnp.concatenate([ids_ref[...], jnp.zeros((top_count, spare), jnp.int32)], axis=1)
+    weights = jnp.concatenate([weights_ref[...], jnp.zeros((top_count, spare), jnp.float32)], axis=1)
+    expert_id = lax.broadcasted_iota(jnp.int32, (LANES, LANES), 0)
+    turned = jnp.zeros((LANES, LANES), jnp.float32)
+    for k in range(top_count):
+        chosen = ids[k : k + 1, :]
+        turned = turned + jnp.where(
+            (expert_id == chosen) | (expert_id == chosen + devices), weights[k : k + 1, :], 0.0
+        )
+    table = turned.T[0:count, :]
     lane = lax.broadcasted_iota(jnp.int32, (count, LANES), 1)
-    table = jnp.zeros((count, LANES), jnp.float32)
-    for k in range(top_count):
-        chosen = ids_ref[:, k : k + 1]
-        table = table + jnp.where(
-            (lane == chosen) | (lane == chosen + devices), weights_ref[:, k : k + 1], 0.0
-        )
     coarse = table.astype(jnp.bfloat16)
     fine = (table - coarse.astype(jnp.float32)).astype(jnp.bfloat16)
     rows_ref[0:count, width : width + LANES] = jnp.where(
         lane < devices, coarse.astype(jnp.float32), fine.astype(jnp.float32)
     ).astype(jnp.bfloat16)
 
-    pl.semaphore_wait(barrier, 3)
+    def normalize(h):
+        part = pl.ds(h * half, half)
+        resid = resid_ref[part, :]
+        mean_square = jnp.mean(resid * resid, axis=-1, keepdims=True)
+        rows_ref[part, 0:width] = (
+            resid * lax.rsqrt(mean_square + 1e-06) * gain_ref[...]
+        ).astype(jnp.bfloat16)
 
     def chunk(s):
         return 0 if s == 0 else 2 * count + (s - 1) * 4 * count
@@ -263,7 +288,7 @@
         return 0 if s == 0 else count + (s - 1) * 2 * count
 
     def half_at(s, direction, h):
-        if s == hops:
+        if s in (0, hops):
             return chunk(s) + h * half
         return chunk(s) + direction * count + h * half
 
@@ -281,7 +306,7 @@
         return s < hops or h == direction
 
     def ring_copy(s, direction, h):
-        source = h * half if s == 1 else half_at(s - 1, direction, h)
+        source = half_at(s - 1, direction, h)
         return remote(
             rows_ref.at[pl.ds(source, half)],
             rows_ref.at[pl.ds(half_at(s, direction, h), half)],
@@ -292,7 +317,7 @@
 
     def pair_copy(s, direction, h):
         start = half_at(s, direction, h)
-        size = count if s == hops else 2 * count
+        size = count if s in (0, hops) else 2 * count
         return remote(
             rows_ref.at[pl.ds(start, half)],
             rows_ref.at[pl.ds(start + size, half)],
@@ -301,23 +326,30 @@
             sibling,
         )
 
-    parts = [(h, direction) for h in range(2) for direction in range(2)]
     sent = []
 
     def go(copy):
         copy.start()
         sent.append(copy)
 
-    for h, direction in parts:
-        go(ring_copy(1, direction, h))
-    home = remote(
-        rows_ref.at[pl.ds(0, count)],
-        rows_ref.at[pl.ds(count, count)],
-        pair_send.at[0, 0, 0],
-        pair_recv.at[0, 0, 0],
-        sibling,
-    )
-    go(home)
+    def home(h):
+        return pair_copy(0, 0, h)
+
+    w_copies = []
+    for h in range(2):
+        for i in range(h * groups // 2, (h + 1) * groups // 2):
+            attend(i)
+        normalize(h)
+        if h == 0:
+            pl.semaphore_wait(barrier, len(others))
+        for direction in range(2):
+            go(ring_copy(1, direction, h))
+        go(home(h))
+        if h == 0:
+            for j, (src, dst) in enumerate(((gate_hbm, gate_ref), (up_hbm, up_ref), (down_hbm, down_ref))):
+                copy = pltpu.make_async_copy(src.at[0], dst, w_sem.at[j])
+                copy.start()
+                w_copies.append(copy)
 
     f_tile = tile_of(hidden_units, 256)
     d_tile = tile_of(width, 512)
@@ -325,30 +357,27 @@
     def expert(start, size):
         span = pl.ds(start, size)
 
-        def first(i, carry):
-            cols = pl.ds(pl.multiple_of(i * f_tile, f_tile), f_tile)
+        def first(i):
+            cols = slice(i * f_tile, (i + 1) * f_tile)
             x = rows_ref[span, 0:width]
             gate = jnp.dot(x, gate_ref[:, cols], preferred_element_type=jnp.float32)
             up = jnp.dot(x, up_ref[:, cols], preferred_element_type=jnp.float32)
             inner_ref[0:size, cols] = (gate / (1.0 + jnp.exp(-gate)) * up).astype(jnp.bfloat16)
-            return carry
-
-        lax.fori_loop(0, hidden_units // f_tile, first, 0)
-        spot = lax.broadcasted_iota(jnp.int32, (size, LANES), 1)
-        both = rows_ref[span, width : width + LANES].astype(jnp.float32)
-        weight = jnp.sum(
-            jnp.where((spot == me) | (spot == me + devices), both, 0.0), axis=-1, keepdims=True
-        )
-
-        def second(i, carry):
-            cols = pl.ds(pl.multiple_of(i * d_tile, d_tile), d_tile)
+
+        def second(i):
+            cols = slice(i * d_tile, (i + 1) * d_tile)
+            spot = lax.broadcasted_iota(jnp.int32, (size, LANES), 1)
+            both = rows_ref[span, width : width + LANES].astype(jnp.float32)
+            weight = jnp.sum(
+                jnp.where((spot == me) | (spot == me + devices), both, 0.0), axis=-1, keepdims=True
+            )
             result = jnp.dot(
                 inner_ref[0:size, :], down_ref[:, cols], preferred_element_type=jnp.float32
             )
             own_ref[span, cols] = (result * weight).astype(jnp.bfloat16)
-            return carry
-
-        lax.fori_loop(0, width // d_tile, second, 0)
+
+        steps = [functools.partial(first, i) for i in range(hidden_units // f_tile)]
+        return steps + [functools.partial(second, i) for i in range(width // d_tile)]
 
     def back_pair(s):
         size = count if s in (0, hops) else 2 * count
@@ -360,25 +389,41 @@
             sibling,
         )
 
-    for s in range(1, hops + 1):
-        moving = [(h, direction) for h, direction in parts if travels(s, direction, h)]
-        for h, direction in moving:
-            ring_copy(s, direction, h).wait_recv()
-            if s < hops and travels(s + 1, direction, h):
-                go(ring_copy(s + 1, direction, h))
-            go(pair_copy(s, direction, h))
+    pending = []
+
+    def run(amount):
+        for _ in range(min(amount, len(pending))):
+            pending.pop(0)()
+
+    def after(s):
         if s == 1:
-            home.wait_recv()
             for copy in w_copies:
                 copy.wait()
-        for h, direction in moving:
-            pair_copy(s, direction, h).wait_recv()
-        if s == 1:
-            expert(0, chunk(2))
-            go(back_pair(0))
-        else:
-            expert(chunk(s), 2 * count if s == hops else 4 * count)
-        go(back_pair(s))
+            for h in range(2):
+                home(h).wait_recv()
+        for h in range(2):
+            for direction in range(2):
+                if travels(s, direction, h):
+                    pair_copy(s, direction, h).wait_recv()
+        if s == hops - 1 and s > 1:
+            return
+        first = 0 if s == 1 else s - 1 if s == hops else s
+        pending.extend(expert(chunk(first), chunk(s) - chunk(first) + (2 if s == hops else 4) * count))
+        for i in range(first, s + 1):
+            pending.append(lambda i=i: go(back_pair(i)))
+
+    for s in range(1, hops + 1):
+        for h in range(2):
+            for direction in range(2):
+                if travels(s, direction, h):
+                    ring_copy(s, direction, h).wait_recv()
+                    if s < hops and travels(s + 1, direction, h):
+                        go(ring_copy(s + 1, direction, h))
+                    go(pair_copy(s, direction, h))
+            run(3)
+        run(len(pending) - 3 if s < hops else len(pending))
+        after(s)
+        run(2 if s < hops else len(pending))
 
     def back_copy(s, direction, h):
         return remote(
@@ -389,23 +434,27 @@
             onward[1 - direction],
         )
 
+    def pass_back(s, direction, h):
+        start = half_at(s, direction, h)
+        offset = start - chunk(s) + own_rows(s)
+        total = own_ref[pl.ds(start, half), :].astype(jnp.float32) + sibling_ref[
+            pl.ds(offset, half), :
+        ].astype(jnp.float32)
+        if s < hops and travels(s + 1, direction, h):
+            back_copy(s + 1, direction, h).wait_recv()
+            total = total + incoming_ref[direction, s, pl.ds(h * half, half), :].astype(jnp.float32)
+        outgoing_ref[direction, s - 1, pl.ds(h * half, half), :] = total.astype(jnp.bfloat16)
+        go(back_copy(s, direction, h))
+
     for s in range(hops, 0, -1):
-        back_pair(s).wait_recv()
-        for h, direction in parts:
-            if not travels(s, direction, h):
-                continue
-            start = half_at(s, direction, h)
-            offset = start - chunk(s) + own_rows(s)
-            total = own_ref[pl.ds(start, half), :].astype(jnp.float32) + sibling_ref[
-                pl.ds(offset, half), :
-            ].astype(jnp.float32)
-            if s < hops and travels(s + 1, direction, h):
-                back_copy(s + 1, direction, h).wait_recv()
-                total = total + incoming_ref[direction, s, pl.ds(h * half, half), :].astype(
-                    jnp.float32
-                )
-            outgoing_ref[direction, s - 1, pl.ds(h * half, half), :] = total.astype(jnp.bfloat16)
-            go(back_copy(s, direction, h))
+        if s == hops:
+            back_pair(s).wait_recv()
+        for direction in range(2):
+            pass_back(s, direction, direction)
+        if s > 1:
+            back_pair(s - 1).wait_recv()
+            for direction in range(2):
+                pass_back(s - 1, direction, 1 - direction)
 
     back_pair(0).wait_recv()
     for h in range(2):
@@ -439,15 +488,22 @@
     hidden_units = w_gate.shape[2]
     hops = devices // 4
     vmem = pl.BlockSpec(memory_space=pltpu.VMEM)
-    hbm = pl.BlockSpec(memory_space=pl.ANY)
+    smem = pl.BlockSpec(memory_space=pltpu.SMEM)
+    hbm = pl.BlockSpec(memory_space=pltpu.HBM)
     dma = pltpu.SemaphoreType.DMA
     bf16 = jnp.bfloat16
+    top_count = expert_ids.shape[1]
     return pl.pallas_call(
         functools.partial(layer_kernel, devices, QUERY_HEADS, KEY_VALUE_HEADS),
         out_shape=jax.ShapeDtypeStruct((count, width), bf16),
-        in_specs=[vmem] * 6 + [hbm] * 5,
+        in_specs=[hbm, hbm, smem] + [hbm] * 8,
         out_specs=vmem,
         scratch_shapes=[
+            pltpu.VMEM((count, width), bf16),
+            pltpu.VMEM((count, width), bf16),
+            pltpu.VMEM((1, width), jnp.float32),
+            pltpu.VMEM((top_count, count), jnp.int32),
+            pltpu.VMEM((top_count, count), jnp.float32),
             pltpu.VMEM(stored_keys.shape, bf16),
             pltpu.VMEM(stored_values.shape, bf16),
             pltpu.VMEM(w_gate.shape[1:], bf16),
@@ -460,6 +516,7 @@
             pltpu.VMEM((devices * count // 2, width), bf16),
             pltpu.VMEM((2, hops, count, width), bf16),
             pltpu.VMEM((2, hops, count, width), bf16),
+            dma((5,)),
             dma((count // GROUP, 2)),
             dma((3,)),
             dma((hops, 2, 2)),
@@ -472,16 +529,16 @@
             dma((hops, 2, 2)),
         ],
         compiler_params=pltpu.CompilerParams(
-            collective_id=0, has_side_effects=True, vmem_limit_bytes=48 * 1024 * 1024
+            collective_id=0, has_side_effects=True, vmem_limit_bytes=60 * 1024 * 1024
         ),
         name="gathered_layer",
     )(
         hidden_in,
         queries,
-        stored_lengths[:, None],
+        stored_lengths,
         norm_gain[None, :],
-        expert_ids,
-        gate_weights,
+        expert_ids.T,
+        gate_weights.T,
         stored_keys,
         stored_values,
         w_gate,
@@ -496,6 +553,7 @@
         and devices % 8 == 0
         and 2 * devices <= LANES
         and count % 32 == 0
+        and count <= LANES
         and 2 * top_count >= devices
     )
 

time: 57.8 us -> 45.7 us (0.79)
  local copies, waits for them, and re-layouts: 9.76 us -> 1.57 us
  Pallas kernels: 47.6 us -> 44 us
    unnamed x15 -> x1, local copies, waits for them, and re-layouts: 9.02 us -> 1.57 us
    pallas_call x1, Pallas kernels: 47.6 us -> 44 us  [gathered_layer(): pl.pallas_call(functools.partial(layer_kernel, devices, QUERY_HEADS, KEY_...]
    broadcast_in_dim x1 -> x0, local copies, waits for them, and re-layouts: 0.74 us -> none  [gathered_layer(): stored_lengths[:, None]]
where the time goes in v3:
time: 45.7 us; the launch traced here: 45.6 us
  Pallas kernels  44 us (96%)
  local copies, waits for them, and re-layouts  1.57 us (3%)
    pallas_call x1, Pallas kernels, gathered_layer(): pl.pallas_call(functools.partial(layer_kernel, devices, QUERY_HEADS, KEY_...  44 us
    unnamed x1, local copies, waits for them, and re-layouts  1.57 us

profile of v3, /device:TPU:0, one launch (start us, length us, event | category | flops | bytes accessed | tf_op | source)
XLA Modules:
  0.0 45.6 jit_solution(14146716613187181381)
XLA Ops:
  0.0 44.0 %gathered_layer.1 = bf16[32,2048]{1,0:T(8,128)(2,1)} custom-call(bf16[32,2048]{1,0:T(8,128)(2,1)} %hidden_hbm.1, bf16[32,2048]{1,0:T(8,128)(2,1)} %queries_hbm.1, s32[32]{0:T(128)} %lengths_ref.1, f32[1,2048]{1,0:T(1,128)} %bitcast.3, s32[8,32]{1,0:T(8,128)} %bitcast.4, f32[8,32]{1,0:T(8,128)} %bitcast.5, bf16[32,64,256]{2,1,0:T(8,128)(2,1)} %keys_hbm.1, ...), custom_call_target="tpu_custom_call" | custom-call | tf_op jit(solution)/shard_map/gathered_layer/pallas_call | solution.py:496
  44.0 1.6 %copy.13 = bf16[32,2048]{1,0:T(8,128)(2,1)} copy(bf16[32,2048]{1,0:T(8,128)(2,1)} %gathered_layer.1) | data formatting | bytes 262144

commit v4 on v3

--- a/solution.py
+++ b/solution.py
@@ -222,8 +222,6 @@
     same_request = (row_id % GROUP) == column_request
     slot_id = col_id % slots
     def attend(i):
-        kv_copies[2 * i].wait()
-        kv_copies[2 * i + 1].wait()
         part = pl.ds(i * GROUP, GROUP)
         lengths = jnp.zeros((square_rows, GROUP * slots), jnp.int32)
         for r in range(GROUP):
@@ -248,8 +246,8 @@
                 * scale
             )
             scores = jnp.where(visible, scores, -1e30)
-            expo = jnp.where(visible, jnp.exp(scores - jnp.max(scores, axis=-1, keepdims=True)), 0.0)
-            probs = (expo / jnp.sum(expo, axis=-1, keepdims=True)).astype(jnp.bfloat16)
+            expo = jnp.exp(scores - jnp.max(scores, axis=-1, keepdims=True))
+            probs = (expo * (1.0 / jnp.sum(expo, axis=-1, keepdims=True))).astype(jnp.bfloat16)
             attended = jnp.dot(probs, v, preferred_element_type=jnp.float32)
             for h in range(per_kv):
                 cols = slice((first + h) * head_size, (first + h + 1) * head_size)
@@ -337,6 +335,8 @@
 
     w_copies = []
     for h in range(2):
+        for copy in kv_copies[h * groups : (h + 1) * groups]:
+            copy.wait()
         for i in range(h * groups // 2, (h + 1) * groups // 2):
             attend(i)
         normalize(h)
@@ -405,9 +405,7 @@
             for direction in range(2):
                 if travels(s, direction, h):
                     pair_copy(s, direction, h).wait_recv()
-        if s == hops - 1 and s > 1:
-            return
-        first = 0 if s == 1 else s - 1 if s == hops else s
+        first = 0 if s == 1 else s
         pending.extend(expert(chunk(first), chunk(s) - chunk(first) + (2 if s == hops else 4) * count))
         for i in range(first, s + 1):
             pending.append(lambda i=i: go(back_pair(i)))
@@ -421,9 +419,9 @@
                         go(ring_copy(s + 1, direction, h))
                     go(pair_copy(s, direction, h))
             run(3)
-        run(len(pending) - 3 if s < hops else len(pending))
+        run(len(pending))
         after(s)
-        run(2 if s < hops else len(pending))
+        run(2 if s < hops - 1 else len(pending))
 
     def back_copy(s, direction, h):
         return remote(
@@ -464,7 +462,7 @@
         for direction in range(2):
             back_copy(1, direction, h).wait_recv()
             total = total + incoming_ref[direction, 0, span, :].astype(jnp.float32)
-        out_ref[span, :] = total.astype(jnp.bfloat16)
+        out_ref[span, :] = total
 
     for copy in sent:
         copy.wait_send()
@@ -495,7 +493,7 @@
     top_count = expert_ids.shape[1]
     return pl.pallas_call(
         functools.partial(layer_kernel, devices, QUERY_HEADS, KEY_VALUE_HEADS),
-        out_shape=jax.ShapeDtypeStruct((count, width), bf16),
+        out_shape=jax.ShapeDtypeStruct((count, width), jnp.float32),
         in_specs=[hbm, hbm, smem] + [hbm] * 8,
         out_specs=vmem,
         scratch_shapes=[
@@ -544,7 +542,7 @@
         w_gate,
         w_up,
         w_down,
-    )
+    ).astype(bf16)
 
 
 def gather_suits(devices, local_experts, count, top_count):

time: 45.7 us -> 45.4 us (level)
  other arithmetic: 0 us -> 1.62 us
  local copies, waits for them, and re-layouts: 1.57 us -> 0 us
    convert_element_type x0 -> x1, other arithmetic: none -> 1.62 us  [gathered_layer(): return pl.pallas_call(functools.partial(layer_kernel, devices, QUERY_HEAD...]
    unnamed x1 -> x0, local copies, waits for them, and re-layouts: 1.57 us -> none
where the time goes in v4:
time: 45.4 us; the launch traced here: 45.2 us
  Pallas kernels  43.6 us (96%)
  other arithmetic  1.62 us (4%)
    pallas_call x1, Pallas kernels, gathered_layer(): pl.pallas_call(functools.partial(layer_kernel, devices, QUERY_HEADS, KEY_...  43.6 us
    convert_element_type x1, other arithmetic, gathered_layer(): return pl.pallas_call(functools.partial(layer_kernel, devices, QUERY_HEAD...  1.62 us

profile of v4, /device:TPU:0, one launch (start us, length us, event | category | flops | bytes accessed | tf_op | source)
XLA Modules:
  0.0 45.2 jit_solution(9039157438637298021)
XLA Ops:
  0.0 43.6 %gathered_layer.1 = f32[32,2048]{1,0:T(8,128)} custom-call(bf16[32,2048]{1,0:T(8,128)(2,1)} %hidden_hbm.1, bf16[32,2048]{1,0:T(8,128)(2,1)} %queries_hbm.1, s32[32]{0:T(128)} %lengths_ref.1, f32[1,2048]{1,0:T(1,128)} %bitcast.3, s32[8,32]{1,0:T(8,128)} %bitcast.4, f32[8,32]{1,0:T(8,128)} %bitcast.5, bf16[32,64,256]{2,1,0:T(8,128)(2,1)} %keys_hbm.1, ...), custom_call_target="tpu_custom_call" | custom-call | tf_op jit(solution)/shard_map/gathered_layer/pallas_call | solution.py:494
  43.6 1.6 %convert_element_type.3 = bf16[32,2048]{1,0:T(8,128)(2,1)} convert(f32[32,2048]{1,0:T(8,128)} %gathered_layer.1) | non-fusion elementwise | flops 65536 | bytes 393216 | tf_op jit(solution)/shard_map/convert_element_type | solution.py:545

commit v5 on v4

--- a/solution.py
+++ b/solution.py
@@ -395,20 +395,22 @@
         for _ in range(min(amount, len(pending))):
             pending.pop(0)()
 
-    def after(s):
-        if s == 1:
-            for copy in w_copies:
-                copy.wait()
+    def arrived(s):
+        if s == 0:
             for h in range(2):
                 home(h).wait_recv()
         for h in range(2):
             for direction in range(2):
-                if travels(s, direction, h):
+                if s > 0 and travels(s, direction, h):
                     pair_copy(s, direction, h).wait_recv()
-        first = 0 if s == 1 else s
-        pending.extend(expert(chunk(first), chunk(s) - chunk(first) + (2 if s == hops else 4) * count))
-        for i in range(first, s + 1):
-            pending.append(lambda i=i: go(back_pair(i)))
+
+    def work(first, last):
+        for s in range(first, last + 1):
+            arrived(s)
+        end = chunk(last) + (2 if last in (0, hops) else 4) * count
+        pending.extend(expert(chunk(first), end - chunk(first)))
+        for s in range(first, last + 1):
+            pending.append(lambda s=s: go(back_pair(s)))
 
     for s in range(1, hops + 1):
         for h in range(2):
@@ -418,10 +420,15 @@
                     if s < hops and travels(s + 1, direction, h):
                         go(ring_copy(s + 1, direction, h))
                     go(pair_copy(s, direction, h))
-            run(3)
-        run(len(pending))
-        after(s)
-        run(2 if s < hops - 1 else len(pending))
+        if s == hops - 1:
+            for copy in w_copies:
+                copy.wait()
+            for first in range(2, hops, 2):
+                work(first, min(first + 1, hops - 1))
+                run(len(pending))
+    work(hops, hops)
+    run(len(pending))
+    work(0, 1)
 
     def back_copy(s, direction, h):
         return remote(
@@ -450,9 +457,12 @@
         for direction in range(2):
             pass_back(s, direction, direction)
         if s > 1:
+            if s == 2:
+                run(len(pending))
             back_pair(s - 1).wait_recv()
             for direction in range(2):
                 pass_back(s - 1, direction, 1 - direction)
+            run(3)
 
     back_pair(0).wait_recv()
     for h in range(2):
@@ -509,7 +519,7 @@
             pltpu.VMEM(w_down.shape[1:], bf16),
             pltpu.VMEM((count, width), jnp.float32),
             pltpu.VMEM((devices * count, width + LANES), bf16),
-            pltpu.VMEM((6 * count, hidden_units), bf16),
+            pltpu.VMEM((8 * count, hidden_units), bf16),
             pltpu.VMEM((devices * count, width), bf16),
             pltpu.VMEM((devices * count // 2, width), bf16),
             pltpu.VMEM((2, hops, count, width), bf16),

time: 45.4 us -> 45.3 us (level)
  no operation moved by 1% of the time
where the time goes in v5:
time: 45.3 us; the launch traced here: 45.1 us
  Pallas kernels  43.4 us (96%)
  other arithmetic  1.62 us (4%)
    pallas_call x1, Pallas kernels, gathered_layer(): pl.pallas_call(functools.partial(layer_kernel, devices, QUERY_HEADS, KEY_...  43.4 us
    convert_element_type x1, other arithmetic, gathered_layer(): return pl.pallas_call(functools.partial(layer_kernel, devices, QUERY_HEAD...  1.62 us

profile of v5, /device:TPU:0, one launch (start us, length us, event | category | flops | bytes accessed | tf_op | source)
XLA Modules:
  0.0 45.1 jit_solution(6144006546255669031)
XLA Ops:
  0.0 43.4 %gathered_layer.1 = f32[32,2048]{1,0:T(8,128)} custom-call(bf16[32,2048]{1,0:T(8,128)(2,1)} %hidden_hbm.1, bf16[32,2048]{1,0:T(8,128)(2,1)} %queries_hbm.1, s32[32]{0:T(128)} %lengths_ref.1, f32[1,2048]{1,0:T(1,128)} %bitcast.3, s32[8,32]{1,0:T(8,128)} %bitcast.4, f32[8,32]{1,0:T(8,128)} %bitcast.5, bf16[32,64,256]{2,1,0:T(8,128)(2,1)} %keys_hbm.1, ...), custom_call_target="tpu_custom_call" | custom-call | tf_op jit(solution)/shard_map/gathered_layer/pallas_call | solution.py:504
  43.5 1.6 %convert_element_type.3 = bf16[32,2048]{1,0:T(8,128)(2,1)} convert(f32[32,2048]{1,0:T(8,128)} %gathered_layer.1) | non-fusion elementwise | flops 65536 | bytes 393216 | tf_op jit(solution)/shard_map/convert_element_type | solution.py:555

commit v6 on v5

--- a/solution.py
+++ b/solution.py
@@ -303,13 +303,18 @@
     def travels(s, direction, h):
         return s < hops or h == direction
 
-    def ring_copy(s, direction, h):
-        source = half_at(s - 1, direction, h)
+    split = width // 2 // LANES * LANES
+
+    def part_of(c, end):
+        return pl.ds(0, split) if c == 0 else pl.ds(split, end - split)
+
+    def ring_copy(s, direction, h, c):
+        cols = part_of(c, width + LANES)
         return remote(
-            rows_ref.at[pl.ds(source, half)],
-            rows_ref.at[pl.ds(half_at(s, direction, h), half)],
-            ring_send.at[s - 1, direction, h],
-            ring_recv.at[s - 1, direction, h],
+            rows_ref.at[pl.ds(half_at(s - 1, direction, h), half), cols],
+            rows_ref.at[pl.ds(half_at(s, direction, h), half), cols],
+            ring_send.at[s - 1, direction, h, c],
+            ring_recv.at[s - 1, direction, h, c],
             onward[direction],
         )
 
@@ -342,8 +347,9 @@
         normalize(h)
         if h == 0:
             pl.semaphore_wait(barrier, len(others))
-        for direction in range(2):
-            go(ring_copy(1, direction, h))
+        for c in range(2):
+            for direction in range(2):
+                go(ring_copy(1, direction, h, c))
         go(home(h))
         if h == 0:
             for j, (src, dst) in enumerate(((gate_hbm, gate_ref), (up_hbm, up_ref), (down_hbm, down_ref))):
@@ -414,12 +420,14 @@
 
     for s in range(1, hops + 1):
         for h in range(2):
-            for direction in range(2):
-                if travels(s, direction, h):
-                    ring_copy(s, direction, h).wait_recv()
-                    if s < hops and travels(s + 1, direction, h):
-                        go(ring_copy(s + 1, direction, h))
-                    go(pair_copy(s, direction, h))
+            for c in range(2):
+                for direction in range(2):
+                    if travels(s, direction, h):
+                        ring_copy(s, direction, h, c).wait_recv()
+                        if s < hops and travels(s + 1, direction, h):
+                            go(ring_copy(s + 1, direction, h, c))
+                        if c == 1:
+                            go(pair_copy(s, direction, h))
         if s == hops - 1:
             for copy in w_copies:
                 copy.wait()
@@ -430,38 +438,44 @@
     run(len(pending))
     work(0, 1)
 
-    def back_copy(s, direction, h):
+    def back_copy(s, direction, h, c):
+        spot = (direction, s - 1, pl.ds(h * half, half), part_of(c, width))
         return remote(
-            outgoing_ref.at[direction, s - 1, pl.ds(h * half, half)],
-            incoming_ref.at[direction, s - 1, pl.ds(h * half, half)],
-            back_send.at[s - 1, direction, h],
-            back_recv.at[s - 1, direction, h],
+            outgoing_ref.at[spot],
+            incoming_ref.at[spot],
+            back_send.at[s - 1, direction, h, c],
+            back_recv.at[s - 1, direction, h, c],
             onward[1 - direction],
         )
 
-    def pass_back(s, direction, h):
+    def pass_back(s, direction, h, c):
+        cols = part_of(c, width)
         start = half_at(s, direction, h)
         offset = start - chunk(s) + own_rows(s)
-        total = own_ref[pl.ds(start, half), :].astype(jnp.float32) + sibling_ref[
-            pl.ds(offset, half), :
+        total = own_ref[pl.ds(start, half), cols].astype(jnp.float32) + sibling_ref[
+            pl.ds(offset, half), cols
         ].astype(jnp.float32)
         if s < hops and travels(s + 1, direction, h):
-            back_copy(s + 1, direction, h).wait_recv()
-            total = total + incoming_ref[direction, s, pl.ds(h * half, half), :].astype(jnp.float32)
-        outgoing_ref[direction, s - 1, pl.ds(h * half, half), :] = total.astype(jnp.bfloat16)
-        go(back_copy(s, direction, h))
+            back_copy(s + 1, direction, h, c).wait_recv()
+            total = total + incoming_ref[direction, s, pl.ds(h * half, half), cols].astype(
+                jnp.float32
+            )
+        outgoing_ref[direction, s - 1, pl.ds(h * half, half), cols] = total.astype(jnp.bfloat16)
+        go(back_copy(s, direction, h, c))
 
     for s in range(hops, 0, -1):
         if s == hops:
             back_pair(s).wait_recv()
-        for direction in range(2):
-            pass_back(s, direction, direction)
+        for c in range(2):
+            for direction in range(2):
+                pass_back(s, direction, direction, c)
         if s > 1:
             if s == 2:
                 run(len(pending))
             back_pair(s - 1).wait_recv()
-            for direction in range(2):
-                pass_back(s - 1, direction, 1 - direction)
+            for c in range(2):
+                for direction in range(2):
+                    pass_back(s - 1, direction, 1 - direction, c)
             run(3)
 
     back_pair(0).wait_recv()
@@ -470,7 +484,8 @@
         total = own_ref[span, :].astype(jnp.float32) + sibling_ref[span, :].astype(jnp.float32)
         total = total + resid_ref[span, :]
         for direction in range(2):
-            back_copy(1, direction, h).wait_recv()
+            for c in range(2):
+                back_copy(1, direction, h, c).wait_recv()
             total = total + incoming_ref[direction, 0, span, :].astype(jnp.float32)
         out_ref[span, :] = total
 
@@ -527,14 +542,14 @@
             dma((5,)),
             dma((count // GROUP, 2)),
             dma((3,)),
-            dma((hops, 2, 2)),
-            dma((hops, 2, 2)),
+            dma((hops, 2, 2, 2)),
+            dma((hops, 2, 2, 2)),
             dma((hops + 1, 2, 2)),
             dma((hops + 1, 2, 2)),
             dma((hops + 1,)),
             dma((hops + 1,)),
-            dma((hops, 2, 2)),
-            dma((hops, 2, 2)),
+            dma((hops, 2, 2, 2)),
+            dma((hops, 2, 2, 2)),
         ],
         compiler_params=pltpu.CompilerParams(
             collective_id=0, has_side_effects=True, vmem_limit_bytes=60 * 1024 * 1024

time: 45.3 us -> 44.6 us (0.985)
  Pallas kernels: 43.4 us -> 42.8 us
    pallas_call x1, Pallas kernels: 43.4 us -> 42.8 us  [gathered_layer(): pl.pallas_call(functools.partial(layer_kernel, devices, QUERY_HEADS, KEY_...]
where the time goes in v6:
time: 44.6 us; the launch traced here: 44.4 us
  Pallas kernels  42.8 us (96%)
  other arithmetic  1.62 us (4%)
    pallas_call x1, Pallas kernels, gathered_layer(): pl.pallas_call(functools.partial(layer_kernel, devices, QUERY_HEADS, KEY_...  42.8 us
    convert_element_type x1, other arithmetic, gathered_layer(): return pl.pallas_call(functools.partial(layer_kernel, devices, QUERY_HEAD...  1.62 us

profile of v6, /device:TPU:0, one launch (start us, length us, event | category | flops | bytes accessed | tf_op | source)
XLA Modules:
  0.0 44.4 jit_solution(7551576174701989715)
XLA Ops:
  0.0 42.8 %gathered_layer.1 = f32[32,2048]{1,0:T(8,128)} custom-call(bf16[32,2048]{1,0:T(8,128)(2,1)} %hidden_hbm.1, bf16[32,2048]{1,0:T(8,128)(2,1)} %queries_hbm.1, s32[32]{0:T(128)} %lengths_ref.1, f32[1,2048]{1,0:T(1,128)} %bitcast.3, s32[8,32]{1,0:T(8,128)} %bitcast.4, f32[8,32]{1,0:T(8,128)} %bitcast.5, bf16[32,64,256]{2,1,0:T(8,128)(2,1)} %keys_hbm.1, ...), custom_call_target="tpu_custom_call" | custom-call | tf_op jit(solution)/shard_map/gathered_layer/pallas_call | solution.py:519
  42.8 1.6 %convert_element_type.3 = bf16[32,2048]{1,0:T(8,128)(2,1)} convert(f32[32,2048]{1,0:T(8,128)} %gathered_layer.1) | non-fusion elementwise | flops 65536 | bytes 393216 | tf_op jit(solution)/shard_map/convert_element_type | solution.py:570

commit v7 on v6

--- a/solution.py
+++ b/solution.py
@@ -385,13 +385,13 @@
         steps = [functools.partial(first, i) for i in range(hidden_units // f_tile)]
         return steps + [functools.partial(second, i) for i in range(width // d_tile)]
 
-    def back_pair(s):
+    def back_pair(s, c):
         size = count if s in (0, hops) else 2 * count
         return remote(
-            own_ref.at[pl.ds(chunk(s) + size, size)],
-            sibling_ref.at[pl.ds(own_rows(s), size)],
-            back_pair_send.at[s],
-            back_pair_recv.at[s],
+            own_ref.at[pl.ds(chunk(s) + size, size), part_of(c, width)],
+            sibling_ref.at[pl.ds(own_rows(s), size), part_of(c, width)],
+            back_pair_send.at[s, c],
+            back_pair_recv.at[s, c],
             sibling,
         )
 
@@ -414,9 +414,12 @@
         for s in range(first, last + 1):
             arrived(s)
         end = chunk(last) + (2 if last in (0, hops) else 4) * count
-        pending.extend(expert(chunk(first), end - chunk(first)))
-        for s in range(first, last + 1):
-            pending.append(lambda s=s: go(back_pair(s)))
+        steps = expert(chunk(first), end - chunk(first))
+        ready = hidden_units // f_tile - (-split // d_tile)
+        for c, some in enumerate((steps[:ready], steps[ready:])):
+            pending.extend(some)
+            for s in range(first, last + 1):
+                pending.append(lambda s=s, c=c: go(back_pair(s, c)))
 
     for s in range(1, hops + 1):
         for h in range(2):
@@ -464,21 +467,22 @@
         go(back_copy(s, direction, h, c))
 
     for s in range(hops, 0, -1):
-        if s == hops:
-            back_pair(s).wait_recv()
         for c in range(2):
+            if s == hops:
+                back_pair(s, c).wait_recv()
             for direction in range(2):
                 pass_back(s, direction, direction, c)
         if s > 1:
             if s == 2:
                 run(len(pending))
-            back_pair(s - 1).wait_recv()
             for c in range(2):
+                back_pair(s - 1, c).wait_recv()
                 for direction in range(2):
                     pass_back(s - 1, direction, 1 - direction, c)
             run(3)
 
-    back_pair(0).wait_recv()
+    for c in range(2):
+        back_pair(0, c).wait_recv()
     for h in range(2):
         span = pl.ds(h * half, half)
         total = own_ref[span, :].astype(jnp.float32) + sibling_ref[span, :].astype(jnp.float32)
@@ -546,8 +550,8 @@
             dma((hops, 2, 2, 2)),
             dma((hops + 1, 2, 2)),
             dma((hops + 1, 2, 2)),
-            dma((hops + 1,)),
-            dma((hops + 1,)),
+            dma((hops + 1, 2)),
+            dma((hops + 1, 2)),
             dma((hops, 2, 2, 2)),
             dma((hops, 2, 2, 2)),
         ],

time: 44.6 us -> 44 us (0.987)
  Pallas kernels: 42.8 us -> 42.2 us
    pallas_call x1, Pallas kernels: 42.8 us -> 42.2 us  [gathered_layer(): pl.pallas_call(functools.partial(layer_kernel, devices, QUERY_HEADS, KEY_...]
where the time goes in v7:
time: 44 us; the launch traced here: 43.8 us
  Pallas kernels  42.2 us (96%)
  other arithmetic  1.62 us (4%)
    pallas_call x1, Pallas kernels, gathered_layer(): pl.pallas_call(functools.partial(layer_kernel, devices, QUERY_HEADS, KEY_...  42.2 us
    convert_element_type x1, other arithmetic, gathered_layer(): return pl.pallas_call(functools.partial(layer_kernel, devices, QUERY_HEAD...  1.62 us

profile of v7, /device:TPU:0, one launch (start us, length us, event | category | flops | bytes accessed | tf_op | source)
XLA Modules:
  0.0 43.8 jit_solution(10836285554474129326)
XLA Ops:
  0.0 42.2 %gathered_layer.1 = f32[32,2048]{1,0:T(8,128)} custom-call(bf16[32,2048]{1,0:T(8,128)(2,1)} %hidden_hbm.1, bf16[32,2048]{1,0:T(8,128)(2,1)} %queries_hbm.1, s32[32]{0:T(128)} %lengths_ref.1, f32[1,2048]{1,0:T(1,128)} %bitcast.3, s32[8,32]{1,0:T(8,128)} %bitcast.4, f32[8,32]{1,0:T(8,128)} %bitcast.5, bf16[32,64,256]{2,1,0:T(8,128)(2,1)} %keys_hbm.1, ...), custom_call_target="tpu_custom_call" | custom-call | tf_op jit(solution)/shard_map/gathered_layer/pallas_call | solution.py:523
  42.2 1.6 %convert_element_type.3 = bf16[32,2048]{1,0:T(8,128)(2,1)} convert(f32[32,2048]{1,0:T(8,128)} %gathered_layer.1) | non-fusion elementwise | flops 65536 | bytes 393216 | tf_op jit(solution)/shard_map/convert_element_type | solution.py:574
